TPU v7x, 256 devices: a whole 4x4x8 slice. The times are simulated.
256 devices in a mesh: dp: 16 (over y, z_hi), expert: 16 (over x, z_lo, core).
Axes of the slice: x: 4, y: 4, z: 8 (z_hi: 4, z_lo: 2; z = z_hi * 2 + z_lo), core: 2. Of those that a mesh axis runs over, the one named last changes fastest.
Arguments:
- tokens: bfloat16 [2048, 4096], P('expert'), may hold values from -6 to 6
- cotangent: bfloat16 [2048, 4096], P('expert', 'dp'), may hold values from -6 to 6
- routes: int32 [2048, 8], P('expert'), may hold values from 0 to 15, all different within a row; in each aligned block of 128 rows (0 to 127, 128 to 255, ...) at most 80 rows name the same one
- router_weight: float32 [2048, 8], P('expert'), may hold values from 0.03 to 0.5
- w_gate: bfloat16 [16, 4096, 2048], P('expert', None, 'dp'), may hold values from -0.09375 to 0.09375
- w_up: bfloat16 [16, 4096, 2048], P('expert', None, 'dp'), may hold values from -0.09375 to 0.09375
- w_down: bfloat16 [16, 2048, 4096], P('expert', None, 'dp'), may hold values from -0.125 to 0.125
- scale_gate: bfloat16 [16, 2048], P('expert', 'dp'), may hold values from 0.5 to 2
- scale_up: bfloat16 [16, 2048], P('expert', 'dp'), may hold values from 0.5 to 2
- scale_down: bfloat16 [16, 4096], P('expert', 'dp'), may hold values from 0.5 to 2
- swapped: int32 [16], replicated, may hold values from 0 to 1, as said below
Outputs:
- mixed: bfloat16 [2048, 4096], P('expert', 'dp')
- grad_gate: bfloat16 [16, 4096, 2048], P('expert', None, 'dp')
- grad_up: bfloat16 [16, 4096, 2048], P('expert', None, 'dp')
- grad_down: bfloat16 [16, 2048, 4096], P('expert', None, 'dp')
- grad_scale_in: bfloat16 [16, 2, 2048], P('expert', None, 'dp')
- grad_scale_out: bfloat16 [16, 4096], P('expert', 'dp')
Inputs may be any that keep to these rules, and one draw needn't show every extreme that they name: `routes`: each row names 8 different experts; among the 128 rows of one device along expert no expert is named by more than 80 rows, a bound that some block reaches. swapped[j] equals swapped[(j + 8) mod 16]; both values occur.
All inputs are finite; a program needn't handle non-finite values.
Results may differ from a plain program's by a relative error of at most 0.0064.
Values may be sent and summed in bfloat16 or wider, within the bound.
A program may use at most 128 MiB of HBM per device.

v0:
```python
import jax
import jax.numpy as jnp
from jax import lax
from jax.sharding import PartitionSpec as P

CAP = 80


def swapped_2(block, axis, stride):
    count = lax.axis_size(axis)
    route = []
    for low in range(count):
        high = low | 1 << stride
        if high != low and high < count:
            route += [(low, high), (high, low)]
    return lax.ppermute(block, axis, route)


def per_device(
    tokens,
    cotangent,
    routes,
    router_weight,
    w_gate,
    w_up,
    w_down,
    scale_gate,
    scale_up,
    scale_down,
    swapped,
):
    holders = lax.axis_size("expert")
    exp_local = w_gate.shape[0]
    num_experts = holders * exp_local
    swap_bit = holders.bit_length() - 2
    my_index = lax.axis_index("expert")
    slot_ids = jnp.arange(num_experts, dtype=jnp.int32)
    my_slots = my_index * exp_local + jnp.arange(exp_local, dtype=jnp.int32)
    local_flag = jnp.sum(
        jnp.where(slot_ids[None, :] == my_slots[:, None], swapped[None, :], 0), axis=1
    )
    flag_three = (local_flag == 1)[:, None, None]
    flag_two = (local_flag == 1)[:, None]
    target = jnp.sum(
        jnp.where(routes[:, :, None] == slot_ids[None, None, :], slot_ids[None, None, :], 0), axis=2
    )
    hit_table = target[:, :, None] == slot_ids[None, None, :]
    routed_mask = jnp.sum(hit_table.astype(jnp.int32), axis=1)
    weight_dense = jnp.sum(jnp.where(hit_table, router_weight[:, :, None], 0.0), axis=1)
    position = jnp.cumsum(routed_mask, axis=0) - routed_mask
    cap_ids = jnp.arange(CAP, dtype=jnp.int32)
    placed = (routed_mask.T[None] == 1) & (position.T[None] == cap_ids[:, None, None])
    weighted = jnp.where(placed, weight_dense.T[None], 0.0)
    placed_b = placed.astype(jnp.bfloat16)
    send_grad = jnp.einsum(
        "cet,td->ced", weighted, cotangent.astype(jnp.float32), precision=lax.Precision.HIGHEST
    ).astype(jnp.bfloat16)
    send_x = jnp.einsum("cet,td->ced", placed_b, tokens, preferred_element_type=jnp.float32).astype(
        jnp.bfloat16
    )
    recv_x, recv_grad = (
        lax.all_to_all(send_x, "expert", split_axis=1, concat_axis=0, tiled=True),
        lax.all_to_all(send_grad, "expert", split_axis=1, concat_axis=0, tiled=True),
    )
    gate_pre = jnp.einsum("rjd,jdf->rjf", recv_x, w_gate, preferred_element_type=jnp.float32)
    up_pre = jnp.einsum("rjd,jdf->rjf", recv_x, w_up, preferred_element_type=jnp.float32)
    gate_scale = scale_gate[None].astype(jnp.float32)
    up_scale = scale_up[None].astype(jnp.float32)
    down_scale = scale_down[None].astype(jnp.float32)
    gate_act = gate_pre * gate_scale
    up_act = up_pre * up_scale
    sigmoid_gate = jax.nn.sigmoid(gate_act)
    silu_gate = gate_act * sigmoid_gate
    hidden = (silu_gate * up_act).astype(jnp.bfloat16)
    down_in = (recv_grad.astype(jnp.float32) * down_scale).astype(jnp.bfloat16)
    piece = lax.all_gather(hidden, "dp", axis=2, tiled=True)
    out_next = jnp.einsum("rjf,jfd->rjd", piece, w_down, preferred_element_type=jnp.float32)
    grad_piece = jnp.einsum("rjf,rjd->jfd", piece, down_in, preferred_element_type=jnp.float32)
    expert_out = (out_next * down_scale).astype(jnp.bfloat16)
    scale_out_grad = jnp.sum(recv_grad.astype(jnp.float32) * out_next, axis=0)
    returned = lax.all_to_all(expert_out, "expert", split_axis=0, concat_axis=1, tiled=True)
    mixed = jnp.einsum(
        "cet,ced->td", weighted, returned.astype(jnp.float32), precision=lax.Precision.HIGHEST
    ).astype(jnp.bfloat16)
    hidden_terms = jnp.einsum("rjd,jfd->rjf", down_in, w_down, preferred_element_type=jnp.float32)
    hidden_grad = lax.psum_scatter(hidden_terms, "dp", scatter_dimension=2, tiled=True)
    gate_grad = hidden_grad * up_act * sigmoid_gate * (1.0 + gate_act * (1.0 - sigmoid_gate))
    up_grad = hidden_grad * silu_gate
    scale_terms = jnp.stack(
        [jnp.sum(gate_grad * gate_pre, axis=0), jnp.sum(up_grad * up_pre, axis=0)], axis=1
    )
    gate_in = (gate_grad * gate_scale).astype(jnp.bfloat16)
    up_in = (up_grad * up_scale).astype(jnp.bfloat16)
    gate_wgrad = jnp.einsum("rjd,rjf->jdf", recv_x, gate_in, preferred_element_type=jnp.float32)
    up_wgrad = jnp.einsum("rjd,rjf->jdf", recv_x, up_in, preferred_element_type=jnp.float32)
    grad_gate = gate_wgrad.astype(jnp.bfloat16)
    grad_up = up_wgrad.astype(jnp.bfloat16)
    grad_down = grad_piece.astype(jnp.bfloat16)
    grad_scale_in = scale_terms.astype(jnp.bfloat16)
    grad_scale_out = scale_out_grad.astype(jnp.bfloat16)
    moved_back = swapped_2(
        (grad_gate, grad_up, grad_down, grad_scale_in, grad_scale_out), "expert", swap_bit
    )
    grad_gate = jnp.where(flag_three, moved_back[0], grad_gate)
    grad_up = jnp.where(flag_three, moved_back[1], grad_up)
    grad_down = jnp.where(flag_three, moved_back[2], grad_down)
    grad_scale_in = jnp.where(flag_three, moved_back[3], grad_scale_in)
    grad_scale_out = jnp.where(flag_two, moved_back[4], grad_scale_out)
    return (mixed, grad_gate, grad_up, grad_down, grad_scale_in, grad_scale_out)


def solution(mesh):
    in_specs = (
        P("expert", None),
        P("expert", "dp"),
        P("expert", None),
        P("expert", None),
        P("expert", None, "dp"),
        P("expert", None, "dp"),
        P("expert", None, "dp"),
        P("expert", "dp"),
        P("expert", "dp"),
        P("expert", "dp"),
        P(),
    )
    out_specs = (
        P("expert", "dp"),
        P("expert", None, "dp"),
        P("expert", None, "dp"),
        P("expert", None, "dp"),
        P("expert", None, "dp"),
        P("expert", "dp"),
    )
    return jax.shard_map(
        per_device, mesh=mesh, in_specs=in_specs, out_specs=out_specs, check_vma=False
    )
```

profile of v0, /device:TPU:1, one launch (start us, length us, event | category | flops | bytes accessed | tf_op | source)
XLA Modules:
  0.0 432.2 jit_solution(15833634414001740296)
XLA Ops:
  7.2 0.8 select_reduce_fusion.1
  8.3 0.7 select_reduce_fusion
  9.1 1.5 convolution_convert_fusion.3
  10.6 1.0 copy.52
  11.7 7.2 %all-to-all-start.2 = ((bf16[80,16,256]{2,0,1:T(8,128)(2,1)}), bf16[80,16,256]{2,0,1:T(8,128)(2,1)S(1)}, u32[]{:S(2)}, u32[]{:S(2)}) async-start(bf16[80,16,256]{2,0,1:T(8,128)(2,1)} %copy.52), calls=%async_computation.2 | async-start | bytes 1310720 | tf_op jit(solution)/shard_map/all_to_all | solution.py:63
  19.6 10.5 %all-to-all-done.2 = bf16[80,16,256]{2,0,1:T(8,128)(2,1)S(1)} async-done(((bf16[80,16,256]{2,0,1:T(8,128)(2,1)}), bf16[80,16,256]{2,0,1:T(8,128)(2,1)S(1)}, u32[]{:S(2)}, u32[]{:S(2)}) %all-to-all-start.2) | async-done | bytes 655392 | tf_op jit(solution)/shard_map/all_to_all | solution.py:63
  30.2 6.8 %convolution_bitcast_fusion = f32[1280,1,2048]{2,0,1:T(8,128)} fusion(bf16[1,2048,256]{2,1,0:T(8,128)(2,1)} %param.17, f32[1280,1,1,1,1,1,256]{6,0,5,4,3,2,1:T(8,128)S(1)} %bitcast.122, f32[256]{0:T(256)S(1)} %bitcast.125), kind=kOutput, calls=%fused_computation | convolution fusion | flops 1342832640 | bytes 12846080 | tf_op jit(solution)/shard_map/rjd,jfd->rjf/dot_general | solution.py:85
  37.0 5.5 %convolution_convert_fusion = bf16[80,16,4096]{2,1,0:T(8,128)(2,1)} fusion(bf16[128,4096]{1,0:T(8,128)(2,1)S(1)} %copy-done, s32[16,128]{1,0:T(8,128)S(1)} %copy.48, pred[16,128]{1,0:T(8,128)(4,1)S(1)} %compare_bitcast_fusion), kind=kOutput, calls=%fused_computation.1 | convolution fusion | flops 1347747840 | bytes 11544576 | tf_op jit(solution)/shard_map/cet,td->ced/dot_general | solution.py:58
  42.5 13.7 %copy.49 = bf16[80,16,4096]{2,0,1:T(8,128)(2,1)} copy(bf16[80,16,4096]{2,1,0:T(8,128)(2,1)} %convolution_convert_fusion) | data formatting | bytes 20971520 | tf_op jit(solution)/shard_map/convert_element_type | solution.py:58
  56.1 5.9 %all-to-all-start = ((bf16[80,16,4096]{2,0,1:T(8,128)(2,1)}), bf16[80,16,4096]{2,0,1:T(8,128)(2,1)}, u32[]{:S(2)}, u32[]{:S(2)}) async-start(bf16[80,16,4096]{2,0,1:T(8,128)(2,1)} %copy.49), calls=%async_computation | async-start | bytes 20971520 | tf_op jit(solution)/shard_map/all_to_all | solution.py:62
  62.3 210.2 %all-to-all-done = bf16[80,16,4096]{2,0,1:T(8,128)(2,1)} async-done(((bf16[80,16,4096]{2,0,1:T(8,128)(2,1)}), bf16[80,16,4096]{2,0,1:T(8,128)(2,1)}, u32[]{:S(2)}, u32[]{:S(2)}) %all-to-all-start) | async-done | bytes 10485792 | tf_op jit(solution)/shard_map/all_to_all | solution.py:62
  272.5 6.4 %convolution_bitcast_fusion.1 = f32[1280,1,128]{2,0,1:T(8,128)} fusion(bf16[1280,4096]{1,0:T(8,128)(2,1)} %bitcast.6, bf16[1,4096,128]{2,1,0:T(8,128)(2,1)S(1)} %copy-done.7), kind=kOutput, calls=%fused_computation.13 | convolution fusion | flops 1342177280 | bytes 12189696 | tf_op jit(solution)/shard_map/rjd,jdf->rjf/dot_general | solution.py:66
  278.9 8.6 %multiply_reduce_fusion.1 = (bf16[128]{0:T(256)(128)(2,1)S(1)}, bf16[128]{0:T(256)(128)(2,1)S(1)}, bf16[1280,1,128]{2,0,1:T(8,128)(2,1)}, f32[1280,1,128]{2,0,1:T(8,128)S(1)}) fusion(f32[128]{0:T(128)S(1)} %get-tuple-element.13, f32[1280,1,128]{2,0,1:T(8,128)} %reduce-scatter.2.cloned.1.call-done, f32[1280,1,128]{2,0,1:T(8,128)} %convolution_bitcast_fusion.1, ...), kind=kOutput, calls=%fused_computation.37 | convolution fusion | flops 1345289984 | bytes 13829632 | tf_op jit(solution)/shard_map/rjd,jdf->rjf/dot_general | solution.py:65
  288.9 0.8 collective-permute-start.3
  289.7 7.1 %fusion.5 = bf16[1,4096,128]{2,1,0:T(8,128)(2,1)S(1)} fusion(bf16[1280,4096]{1,0:T(8,128)(2,1)} %bitcast.6, f32[128]{0:T(128)S(1)} %get-tuple-element.12, f32[1280,1,128]{2,0,1:T(8,128)S(1)} %copy-done.8, f32[1280,1,128]{2,0,1:T(8,128)S(1)} %get-tuple-element.11, f32[128]{0:T(128)S(1)} %get-tuple-element.13), kind=kOutput, calls=%fused_computation.9 | convolution fusion | flops 1344012288 | bytes 12846080 | tf_op jit(solution)/shard_map/rjd,rjf->jdf/dot_general | solution.py:95
  296.8 2.3 collective-permute-start.1
  299.1 8.1 %fusion.4 = bf16[1,4096,128]{2,1,0:T(8,128)(2,1)} fusion(bf16[1280,4096]{1,0:T(8,128)(2,1)} %bitcast.6, f32[128]{0:T(128)S(1)} %get-tuple-element.13, f32[1280,1,128]{2,0,1:T(8,128)S(1)} %copy-done.8, f32[1280,1,128]{2,0,1:T(8,128)S(1)} %copy-done.10, f32[1280,1,128]{2,0,1:T(8,128)} %copy-done.11, f32[128]{0:T(128)S(1)} %get-tuple-element.12), kind=kOutput, calls=%fused_computation.8 | convolution fusion | flops 1344831488 | bytes 13501440 | tf_op jit(solution)/shard_map/rjd,rjf->jdf/dot_general | solution.py:94
  307.2 1.0 collective-permute-start
  308.7 13.6 %collective-permute-done.1 = bf16[1,4096,128]{2,1,0:T(8,128)(2,1)S(1)} collective-permute-done((bf16[1,4096,128]{2,1,0:T(8,128)(2,1)S(1)}, bf16[1,4096,128]{2,1,0:T(8,128)(2,1)S(1)}, u32[]{:S(2)}, u32[]{:S(2)}) %collective-permute-start.1) | collective-permute-done | bytes 1048608 | tf_op jit(solution)/shard_map/ppermute | solution.py:16
  322.3 1.1 broadcast_select_fusion.1
  323.4 55.5 %all-gather.2.cloned.1.call-done = bf16[1280,1,2048]{2,0,1:T(8,128)(2,1)} async-done(((bf16[1280,1,128]{2,0,1:T(8,128)(2,1)}), bf16[1280,1,2048]{2,0,1:T(8,128)(2,1)}) %all-gather.2.cloned.1.call-update) | async-done | bytes 5242896 | tf_op jit(solution)/shard_map/all_gather | solution.py:76
  378.9 5.0 %fusion.15 = (bf16[256]{0:T(256)(128)(2,1)S(1)}, bf16[1280,1,256]{2,0,1:T(8,128)(2,1)}) fusion(f32[80,16,1,256]{3,0,1,2:T(8,128)S(1)} %bitcast_convert_fusion, f32[256]{0:T(256)S(1)} %bitcast.126, bf16[1,2048,256]{2,1,0:T(8,128)(2,1)S(1)} %copy-done.2, bf16[1280,1,2048]{2,0,1:T(8,128)(2,1)} %all-gather.2.cloned.1.call-done), kind=kOutput, calls=%fused_computation.17 | convolution fusion | flops 1343487744 | bytes 8259072 | tf_op jit(solution)/shard_map/rjf,jfd->rjd/dot_general | solution.py:77
  383.9 2.8 collective-permute-start.4
  386.7 2.7 fusion.12
  390.2 1.1 reduce.5
  391.3 1.0 reshape.262
  392.4 5.3 %all-to-all-start.1 = ((bf16[16,2,10240]{2,1,0:T(2,128)(2,1)}), bf16[16,2,10240]{2,1,0:T(2,128)(2,1)S(1)}, u32[]{:S(2)}, u32[]{:S(2)}) async-start(bf16[16,2,10240]{2,1,0:T(2,128)(2,1)} %reshape.262), calls=%async_computation.1 | async-start | bytes 1310720 | tf_op jit(solution)/shard_map/all_to_all | solution.py:81
  397.7 2.4 broadcast_select_fusion.2
  400.6 18.0 %collective-permute-done.2 = bf16[1,2048,256]{2,1,0:T(8,128)(2,1)S(1)} collective-permute-done((bf16[1,2048,256]{2,1,0:T(8,128)(2,1)}, bf16[1,2048,256]{2,1,0:T(8,128)(2,1)S(1)}, u32[]{:S(2)}, u32[]{:S(2)}) %collective-permute-start.2) | collective-permute-done | bytes 1048608 | tf_op jit(solution)/shard_map/ppermute | solution.py:16
  418.6 2.3 broadcast_select_fusion
  420.9 2.1 all-to-all-done.1
  423.8 1.5 fusion.16
  (50 shorter events, 4.8 us)
Async XLA Ops:
  7.2 29.8 %copy-start = (bf16[128,4096]{1,0:T(8,128)(2,1)S(1)}, bf16[128,4096]{1,0:T(8,128)(2,1)}, u32[]{:S(2)}) copy-start(bf16[128,4096]{1,0:T(8,128)(2,1)} %param.11) | copy-start | bytes 3145732
  11.7 18.4 %all-to-all-start.2 = ((bf16[80,16,256]{2,0,1:T(8,128)(2,1)}), bf16[80,16,256]{2,0,1:T(8,128)(2,1)S(1)}, u32[]{:S(2)}, u32[]{:S(2)}) async-start(bf16[80,16,256]{2,0,1:T(8,128)(2,1)} %copy.52), calls=%async_computation.2 | async-start | bytes 1310720 | tf_op jit(solution)/shard_map/all_to_all | solution.py:63
  18.8 260.1 %reduce-scatter.2.cloned.1.call-start = ((), (), s32[]{:S(2)}) async-start(), calls=%async_computation.5 | async-start | bytes 11141120 | tf_op jit(solution)/shard_map/reduce_scatter | solution.py:86
  56.1 6.1 %copy-start.4 = (bf16[1,128]{1,0:T(2,128)(2,1)S(1)}, bf16[1,128]{1,0:T(2,128)(2,1)}, u32[]{:S(2)}) copy-start(bf16[1,128]{1,0:T(2,128)(2,1)} %param.19) | copy-start | bytes 772
  56.1 6.1 %copy-start.5 = (bf16[1,128]{1,0:T(2,128)(2,1)S(1)}, bf16[1,128]{1,0:T(2,128)(2,1)}, u32[]{:S(2)}) copy-start(bf16[1,128]{1,0:T(2,128)(2,1)} %param.18) | copy-start | bytes 772
  56.1 216.3 %copy-start.7 = (bf16[1,4096,128]{2,1,0:T(8,128)(2,1)S(1)}, bf16[1,4096,128]{2,1,0:T(8,128)(2,1)}, u32[]{:S(2)}) copy-start(bf16[1,4096,128]{2,1,0:T(8,128)(2,1)} %param.16) | copy-start | bytes 3145732
  56.1 216.3 %all-to-all-start = ((bf16[80,16,4096]{2,0,1:T(8,128)(2,1)}), bf16[80,16,4096]{2,0,1:T(8,128)(2,1)}, u32[]{:S(2)}, u32[]{:S(2)}) async-start(bf16[80,16,4096]{2,0,1:T(8,128)(2,1)} %copy.49), calls=%async_computation | async-start | bytes 20971520 | tf_op jit(solution)/shard_map/all_to_all | solution.py:62
  62.0 316.9 %all-gather.2.cloned.1.call-start = ((), (), s32[]{:S(2)}) async-start(), calls=%async_computation.4 | async-start | bytes 5570560 | tf_op jit(solution)/shard_map/all_gather | solution.py:76
  278.9 8.6 %copy-start.9 = (s32[16]{0:T(128)S(1)}, s32[16]{0:T(128)}, u32[]{:S(2)}) copy-start(s32[16]{0:T(128)} %param.21) | copy-start | bytes 196
  278.9 10.8 %copy-start.8 = (f32[1280,1,128]{2,0,1:T(8,128)S(1)}, f32[1280,1,128]{2,0,1:T(8,128)}, u32[]{:S(2)}) copy-start(f32[1280,1,128]{2,0,1:T(8,128)} %reduce-scatter.2.cloned.1.call-done) | copy-start | bytes 1966084
  287.5 2.2 copy-start.11
  288.9 19.3 %collective-permute-start.3 = (bf16[1,2,128]{2,1,0:T(2,128)(2,1)S(1)}, bf16[1,2,128]{2,1,0:T(2,128)(2,1)S(1)}, u32[]{:S(2)}, u32[]{:S(2)}) collective-permute-start(bf16[1,2,128]{2,1,0:T(2,128)(2,1)S(1)} %pad_maximum_fusion), channel_id=1, source_target_pairs={{0,8},{8,0},{1,9},{9,1},{2,10},{10,2},{3,11},{11,3},{4,12},{12,4},... | collective-permute-start | bytes 1544 | tf_op jit(solution)/shard_map/ppermute | solution.py:16
  289.7 9.4 %copy-start.10 = (f32[1280,1,128]{2,0,1:T(8,128)S(1)}, f32[1280,1,128]{2,0,1:T(8,128)}, u32[]{:S(2)}) copy-start(f32[1280,1,128]{2,0,1:T(8,128)} %convolution_bitcast_fusion.1) | copy-start | bytes 1966084
  296.7 82.2 %copy-start.2 = (bf16[1,2048,256]{2,1,0:T(8,128)(2,1)S(1)}, bf16[1,2048,256]{2,1,0:T(8,128)(2,1)}, u32[]{:S(2)}) copy-start(bf16[1,2048,256]{2,1,0:T(8,128)(2,1)} %param.17) | copy-start | bytes 3145732
  296.8 25.6 %collective-permute-start.1 = (bf16[1,4096,128]{2,1,0:T(8,128)(2,1)S(1)}, bf16[1,4096,128]{2,1,0:T(8,128)(2,1)S(1)}, u32[]{:S(2)}, u32[]{:S(2)}) collective-permute-start(bf16[1,4096,128]{2,1,0:T(8,128)(2,1)S(1)} %fusion.5), channel_id=1, source_target_pairs={{0,8},{8,0},{1,9},{9,1},{2,10},{10,2},{3,11},{11,3},{4,12},{12,4},... | collective-permute-start | bytes 3145736 | tf_op jit(solution)/shard_map/ppermute | solution.py:16
  307.2 90.4 %collective-permute-start = (bf16[1,4096,128]{2,1,0:T(8,128)(2,1)}, bf16[1,4096,128]{2,1,0:T(8,128)(2,1)}, u32[]{:S(2)}, u32[]{:S(2)}) collective-permute-start(bf16[1,4096,128]{2,1,0:T(8,128)(2,1)} %fusion.4), channel_id=1, source_target_pairs={{0,8},{8,0},{1,9},{9,1},{2,10},{10,2},{3,11},{11,3},{4,12},{12,4},... | collective-permute-start | bytes 3145736 | tf_op jit(solution)/shard_map/ppermute | solution.py:16
  378.9 7.8 %copy-start.6 = (bf16[1280,1,2048]{2,0,1:T(8,128)(2,1)S(1)}, bf16[1280,1,2048]{2,0,1:T(8,128)(2,1)}, u32[]{:S(2)}) copy-start(bf16[1280,1,2048]{2,0,1:T(8,128)(2,1)} %all-gather.2.cloned.1.call-done) | copy-start | bytes 15728644
  383.9 6.3 %copy-start.3 = (bf16[1280,1,256]{2,0,1:T(8,128)(2,1)S(1)}, bf16[1280,1,256]{2,0,1:T(8,128)(2,1)}, u32[]{:S(2)}) copy-start(bf16[1280,1,256]{2,0,1:T(8,128)(2,1)} %get-tuple-element.10) | copy-start | bytes 1966084
  383.9 16.1 %collective-permute-start.4 = (bf16[1,256]{1,0:T(2,128)(2,1)S(1)}, bf16[1,256]{1,0:T(2,128)(2,1)S(1)}, u32[]{:S(2)}, u32[]{:S(2)}) collective-permute-start(bf16[1,256]{1,0:T(2,128)(2,1)S(1)} %convert_element_type.204), channel_id=1, source_target_pairs={{0,8},{8,0},{1,9},{9,1},{2,10},{10,2},{3,11},{11,3},{4,12},{12,4},... | collective-permute-start | bytes 1544 | tf_op jit(solution)/shard_map/ppermute | solution.py:16
  389.4 29.2 %collective-permute-start.2 = (bf16[1,2048,256]{2,1,0:T(8,128)(2,1)}, bf16[1,2048,256]{2,1,0:T(8,128)(2,1)S(1)}, u32[]{:S(2)}, u32[]{:S(2)}) collective-permute-start(bf16[1,2048,256]{2,1,0:T(8,128)(2,1)} %fusion.12), channel_id=1, source_target_pairs={{0,8},{8,0},{1,9},{9,1},{2,10},{10,2},{3,11},{11,3},{4,12},{12,4},... | collective-permute-start | bytes 3145736 | tf_op jit(solution)/shard_map/ppermute | solution.py:16
  392.4 30.7 %all-to-all-start.1 = ((bf16[16,2,10240]{2,1,0:T(2,128)(2,1)}), bf16[16,2,10240]{2,1,0:T(2,128)(2,1)S(1)}, u32[]{:S(2)}, u32[]{:S(2)}) async-start(bf16[16,2,10240]{2,1,0:T(2,128)(2,1)} %reshape.262), calls=%async_computation.1 | async-start | bytes 1310720 | tf_op jit(solution)/shard_map/all_to_all | solution.py:81
  397.6 27.7 %copy-start.1 = (bf16[128,4096]{1,0:T(8,128)(2,1)S(1)}, bf16[128,4096]{1,0:T(8,128)(2,1)}, u32[]{:S(2)}) copy-start(bf16[128,4096]{1,0:T(8,128)(2,1)} %param.11) | copy-start | bytes 3145732
Sparse Core Ops, SparseCore 0:
  37.1 184.3 reduce-scatter.1
  287.6 91.2 all-gather.1
where the time goes:
time: 433 us; the launch traced here: 432 us
  waiting for transfers between devices  310 us (72%)
  matrix products  53.1 us (12%)
  starting transfers between devices  25.8 us (6%)
  local copies, waits for them, and re-layouts  17.2 us (4%)
  between operations  14.8 us (3%)
  other arithmetic  11.2 us (3%)
    all_to_all x1, waiting for transfers between devices, per_device(): lax.all_to_all(send_x, 'expert', split_axis=1, concat_axis=0, tiled=True)  210 us
    all_gather x1, waiting for transfers between devices, per_device(): piece = lax.all_gather(hidden, 'dp', axis=2, tiled=True)  55.5 us
    ppermute x5, waiting for transfers between devices, swapped_2(): return lax.ppermute(block, axis, route)  31.6 us
    convert_element_type x1, local copies, waits for them, and re-layouts, per_device(): jnp.einsum('cet,td->ced', placed_b, tokens, preferred_element_type=jnp.fl...  13.7 us
    all_to_all x1, waiting for transfers between devices, per_device(): lax.all_to_all(send_grad, 'expert', split_axis=1, concat_axis=0, tiled=True)  10.5 us
  transfers between devices with their start and end apart: 10, of which 6 were waited for; matrix products, arithmetic and copies ran while one was open for 14% of the time, Pallas kernels for 0%

commit v1 on v0

v1 whole, which is shorter than its diff:
```python
import jax
import jax.numpy as jnp
from jax import lax
from jax.experimental import pallas as pl
from jax.experimental.pallas import tpu as pltpu
from jax.sharding import PartitionSpec as P

MESH = pl.DeviceIdType.MESH
BF = jnp.bfloat16
F32 = jnp.float32
CAP = 80
BLK = 16
TOK = 128
D = 4096
ROWS = BLK * CAP
NCH = 4
CROWS = ROWS // NCH
TCH = 4
ZFIRST = (0,)
VMEM_LIMIT = 60 * 2**20
NT = (((1,), (1,)), ((), ()))
TN = (((0,), (0,)), ((), ()))


def place():
    dp = lax.axis_index("dp")
    ex = lax.axis_index("expert")
    y, zh = lax.div(dp, 4), lax.rem(dp, 4)
    x, zl, c = lax.div(ex, 4), lax.rem(lax.div(ex, 2), 2), lax.rem(ex, 2)
    return x, y, zh * 2 + zl, c


def device(x, y, z, c):
    x, y, z, c = lax.rem(x + 4, 4), lax.rem(y + 4, 4), lax.rem(z + 8, 8), lax.rem(c + 2, 2)
    return (y * 4 + lax.div(z, 2), slot(x, z, c))


def slot(x, z, c):
    return lax.rem(x + 4, 4) * 4 + lax.rem(z + 8, 2) * 2 + c


class Links:
    def __init__(self, send_sems, recv_sems, other):
        self.ss, self.rs, self.other = send_sems, recv_sems, other
        self.copies = []

    def send(self, src, dst, to):
        i = len(self.copies)
        copy = pltpu.make_async_remote_copy(
            src_ref=src,
            dst_ref=dst,
            send_sem=self.ss.at[i],
            recv_sem=self.rs.at[i],
            device_id=to,
            device_id_type=MESH,
        )
        copy.start()
        self.copies.append(copy)
        return i

    def arrived(self, i, dst):
        pltpu.make_async_remote_copy(
            src_ref=dst,
            dst_ref=dst,
            send_sem=self.ss.at[i],
            recv_sem=self.rs.at[i],
            device_id=self.other,
            device_id_type=MESH,
        ).wait_recv()

    def finish(self):
        for copy in self.copies:
            copy.wait_send()


def greet(devices):
    barrier = pltpu.get_barrier_semaphore()
    for to in devices:
        pl.semaphore_signal(barrier, inc=1, device_id=to, device_id_type=MESH)
    pl.semaphore_wait(barrier, len(devices))


def gather_kernel(
    comb, cot, tok, wd, sd,
    toks, rg, di4, wd4, hg, cw_own, cw_par,
    cots, combs, pos, part, rz, ss, rs, local,
):
    x, y, z, c = place()
    zl = lax.rem(z, 2)
    zh = lax.div(z, 2)
    me = slot(x, z, c)
    sibling = device(x, y, z, 1 - c)
    chip = x * 2 + zl
    links = Links(ss, rs, sibling)

    def chip_at(k):
        q = lax.rem(chip + k + 8, 8)
        qx, qz = lax.div(q, 2), lax.rem(q, 2)
        return qx, zh * 2 + qz

    peers = [sibling]
    for k in range(1, 8):
        qx, qz = chip_at(k)
        peers.append(device(qx, y, qz, c))
    far_z = z - 1 + 2 * zl
    peers.append(device(x, y, far_z, c))
    for d in range(1, 4):
        peers.append(device(x, y + d, z, c))
        peers.append(device(x, y, z + 2 * d, c))
    greet(peers)

    first = []
    for k in range(1, 8):
        to = peers[k]
        first.append((k, links.send(comb, combs.at[me], to), links.send(cot, cots.at[me], to)))
    over = [(0, links.send(comb, combs.at[me], sibling), links.send(cot, cots.at[me], sibling))]
    wd_ids = []
    for d in (1, 3, 2):
        to_y = lax.rem(y + d, 4)
        rows = pl.ds(pl.multiple_of(to_y * 512, 512), 512)
        wd_ids.append((d, links.send(wd.at[rows], wd4.at[y], device(x, y + d, z, c))))
    own_tok = pltpu.make_async_copy(tok, toks.at[me], local.at[0])
    own_tok.start()
    combs[me] = comb[...]
    cots[me] = cot[...]
    wd4[y] = wd[pl.ds(pl.multiple_of(y * 512, 512), 512), :]
    for k, ia, ib in first:
        qx, qz = chip_at(-k)
        s = slot(qx, qz, c)
        links.arrived(ia, combs.at[s])
        links.arrived(ib, cots.at[s])
        over.append((k, links.send(combs.at[s], combs.at[s], sibling), links.send(cots.at[s], cots.at[s], sibling)))

    rt = TOK // TCH
    half = rt // 2

    def rows_of(k):
        return pl.ds(k * rt, rt)

    def low(k):
        return pl.ds(k * rt, half)

    def high(k):
        return pl.ds(k * rt + half, half)

    pair = []
    pair.append((links.send(tok, toks.at[me], sibling), lambda: toks.at[slot(x, z, 1 - c)]))
    xs, zs = {}, {}
    up, down = device(x, y, z + 1, c), device(x, y, z - 1, c)
    for k in range(TCH):
        for d in (1, 3, 2):
            xs[k, d] = links.send(tok.at[rows_of(k)], toks.at[me, rows_of(k)], device(x + d, y, z, c))
        zs[k, 0] = (
            links.send(tok.at[low(k)], toks.at[me, low(k)], up),
            links.send(tok.at[high(k)], toks.at[me, high(k)], down),
        )

    def to_sibling(sx, sz, k):
        s = slot(sx, sz, c)
        other = slot(sx, sz, 1 - c)
        i = links.send(toks.at[s, rows_of(k)], toks.at[s, rows_of(k)], sibling)
        pair.append((i, lambda: toks.at[other, rows_of(k)]))

    def x_event(k):
        for d in (1, 3, 2):
            s = slot(x - d, z, c)
            links.arrived(xs[k, d], toks.at[s, rows_of(k)])
            if k not in ZFIRST:
                zs[k, d] = (
                    links.send(toks.at[s, low(k)], toks.at[s, low(k)], up),
                    links.send(toks.at[s, high(k)], toks.at[s, high(k)], down),
                )
            to_sibling(x - d, z, k)

    def z_arrive(k, d):
        s = slot(x - d, z + 1, c)
        links.arrived(zs[k, d][0], toks.at[s, low(k)])
        links.arrived(zs[k, d][1], toks.at[s, high(k)])
        to_sibling(x - d, z + 1, k)
        return s

    x2 = {}

    def z_event(k):
        if k in ZFIRST:
            s = z_arrive(k, 0)
            for d in (1, 3, 2):
                x2[k, d] = links.send(toks.at[s, rows_of(k)], toks.at[s, rows_of(k)], device(x + d, y, z, c))
        else:
            for d in (0, 1, 3, 2):
                z_arrive(k, d)

    def x2_event(k):
        for d in (1, 3, 2):
            s = slot(x - d, z + 1, c)
            links.arrived(x2[k, d], toks.at[s, rows_of(k)])
            to_sibling(x - d, z + 1, k)

    for k, ia, ib in over:
        qx, qz = chip_at(-k)
        s = slot(qx, qz, 1 - c)
        links.arrived(ia, combs.at[s])
        links.arrived(ib, cots.at[s])

    experts = lax.broadcasted_iota(jnp.int32, (BLK, BLK, TOK), 1)
    table = combs[...]
    cw = jnp.sum(jnp.where(experts == me, table, 0.0), axis=1)
    cw_own[...] = cw
    cw_par[...] = jnp.sum(jnp.where(experts == lax.rem(me + 8, 16), table, 0.0), axis=1)
    before = lax.broadcasted_iota(jnp.int32, (TOK, TOK), 0) < lax.broadcasted_iota(jnp.int32, (TOK, TOK), 1)
    pos[...] = jnp.dot((cw > 0).astype(BF), before.astype(F32).astype(BF), preferred_element_type=F32)
    spots = lax.broadcasted_iota(jnp.int32, (CAP, TOK), 0).astype(F32)
    scale = sd[...].astype(F32)

    def compact(r, _):
        weight = cw_own[pl.ds(r, 1), :]
        hit = (pos[pl.ds(r, 1), :] == spots) & (weight > 0)
        picked = jnp.dot(jnp.where(hit, 1.0, 0.0).astype(BF), cots[r], preferred_element_type=F32)
        w = jnp.sum(jnp.where(hit, weight, 0.0), axis=1, keepdims=True)
        routed = (picked * w).astype(BF)
        rows = pl.ds(pl.multiple_of(r * CAP, CAP), CAP)
        rg[rows, :] = routed
        di4[y, rows, :] = (routed.astype(F32) * scale).astype(BF)
        return 0

    ys = {}
    for i in range(NCH):
        lax.fori_loop(i * (BLK // NCH), (i + 1) * (BLK // NCH), compact, 0)
        rows = pl.ds(i * CROWS, CROWS)
        for d in (1, 3, 2):
            ys[i, d] = links.send(di4.at[y, rows], di4.at[y, rows], device(x, y + d, z, c))
    for d, i in wd_ids:
        links.arrived(i, wd4.at[lax.rem(y - d + 4, 4)])

    zr = {}

    def terms(i):
        rows = pl.ds(i * CROWS, CROWS)
        for d in (1, 3, 2):
            links.arrived(ys[i, d], di4.at[lax.rem(y - d + 4, 4), rows])
        acc = lax.dot_general(di4[0, rows, :], wd4[0], NT, preferred_element_type=F32)
        for j in range(1, 4):
            acc += lax.dot_general(di4[j, rows, :], wd4[j], NT, preferred_element_type=F32)
        acc = acc.astype(BF)
        for j in range(4):
            part[j, rows, :] = acc[:, j * 128:(j + 1) * 128]
        for d in (2, 1, 3):
            zr[i, d] = links.send(part.at[lax.rem(zh + d, 4), rows], rz.at[d - 1, rows], device(x, y, z + 2 * d, c))

    def gradient(i):
        rows = pl.ds(i * CROWS, CROWS)
        for d in (1, 2, 3):
            links.arrived(zr[i, d], rz.at[d - 1, rows])
        total = part[zh, rows, :].astype(F32)
        for d in (1, 2, 3):
            total += rz[d - 1, rows, :].astype(F32)
        hg[rows, :] = total

    for i in range(NCH):
        terms(i)
        if i in ZFIRST:
            z_event(i)
        x_event(i)
    for i in range(NCH):
        if i in ZFIRST:
            x2_event(i)
        else:
            z_event(i)
    for i in range(NCH):
        gradient(i)
    for i, where in pair:
        links.arrived(i, where())
    own_tok.wait()
    links.finish()


def gather(comb, cot, tok, wd, sd):
    n = 170
    vm = pl.BlockSpec(memory_space=pltpu.VMEM)
    hbm = pl.BlockSpec(memory_space=pl.ANY)
    return pl.pallas_call(
        gather_kernel,
        out_shape=(
            jax.ShapeDtypeStruct((BLK, TOK, D), BF),
            jax.ShapeDtypeStruct((ROWS, 256), BF),
            jax.ShapeDtypeStruct((4, ROWS, 256), BF),
            jax.ShapeDtypeStruct((4, 512, 256), BF),
            jax.ShapeDtypeStruct((ROWS, 128), F32),
            jax.ShapeDtypeStruct((BLK, TOK), F32),
            jax.ShapeDtypeStruct((BLK, TOK), F32),
        ),
        in_specs=[vm, vm, hbm, vm, vm],
        out_specs=(hbm, vm, vm, vm, vm, vm, vm),
        scratch_shapes=[
            pltpu.VMEM((BLK, TOK, 256), BF),
            pltpu.VMEM((BLK, BLK, TOK), F32),
            pltpu.VMEM((BLK, TOK), F32),
            pltpu.VMEM((4, ROWS, 128), BF),
            pltpu.VMEM((3, ROWS, 128), BF),
            pltpu.SemaphoreType.DMA((n,)),
            pltpu.SemaphoreType.DMA((n,)),
            pltpu.SemaphoreType.DMA((1,)),
        ],
        name="gather",
        compiler_params=pltpu.CompilerParams(collective_id=0, has_side_effects=True, vmem_limit_bytes=VMEM_LIMIT),
    )(comb, cot, tok, wd, sd)


def down_kernel(
    hid, gi, sc, comb, comb_t, rg, di4, wd4, sd,
    mixed, own_gd, far_gd, gi_far, sc_far, so_own, so_far,
    hz, op, ro, eo, ret, gd, so, ss, rs,
):
    x, y, z, c = place()
    zh = lax.div(z, 2)
    me = slot(x, z, c)
    far = device(x + 2, y, z, c)
    links = Links(ss, rs, far)
    peers = []
    for k in range(1, 16):
        e = lax.rem(me + k, 16)
        peers.append((lax.axis_index("dp"), e))
    for d in range(1, 4):
        peers.append(device(x, y + d, z, c))
        peers.append(device(x, y, z + 2 * d, c))
        peers.append(device(x + 2, y + d, z, c))
    greet(peers)

    columns = pl.ds(pl.multiple_of(zh * 128, 128), 128)
    zs = {}
    order = [lax.rem(x + 1 + i, 4) for i in range(NCH)]

    def chunk(i):
        return pl.ds(pl.multiple_of(order[i] * CROWS, CROWS), CROWS)

    for i in range(NCH):
        rows = chunk(i)
        for d in (2, 1, 3):
            zs[i, d] = links.send(hid.at[rows], hz.at[rows, columns], device(x, y, z + 2 * d, c))
    gi_id = links.send(gi, gi_far, far)
    sc_id = links.send(sc, sc_far, far)
    hz[:, columns] = hid[...]

    ys = {}

    def project(i):
        rows = chunk(i)
        for d in (1, 3, 2):
            from_z = lax.rem(zh - d + 4, 4)
            links.arrived(zs[i, d], hz.at[rows, pl.ds(pl.multiple_of(from_z * 128, 128), 128)])
        left = hz[rows, :]
        for d in (2, 1, 3, 0):
            j = lax.rem(y + d, 4)
            op[j, rows, :] = jnp.dot(left, wd4[j], preferred_element_type=F32).astype(BF)
            if d:
                ys[i, d] = links.send(op.at[j, rows], ro.at[d - 1, rows], device(x, y + d, z, c))

    scale = sd[...].astype(F32)
    so[...] = jnp.zeros_like(so)
    back = {}
    inner = lax.rem(me, 4)

    def give(i):
        rows = chunk(i)
        for d in (1, 3, 2):
            links.arrived(ys[i, d], ro.at[d - 1, rows])
        total = op[y, rows, :].astype(F32)
        for d in (1, 2, 3):
            total += ro[d - 1, rows, :].astype(F32)
        so[0:1, :] += jnp.sum(total * rg[rows, :].astype(F32), axis=0, keepdims=True)
        eo[rows, :] = (total * scale).astype(BF)
        for j in range(4):
            r = order[i] * 4 + lax.rem(inner + j, 4)
            block = pl.ds(pl.multiple_of(r * CAP, CAP), CAP)
            if i == NCH - 1 and j == 0:
                ret[me] = eo[block, :]
            else:
                back[i, j] = links.send(eo.at[block], ret.at[me], (lax.axis_index("dp"), r))

    project(0)
    for i in range(1, NCH):
        project(i)
        give(i - 1)
    gds = {}
    for d in (1, 2, 3, 0):
        j = lax.rem(y + d, 4)
        gd[j] = lax.dot_general(hz[...], di4[j], TN, preferred_element_type=F32).astype(BF)
        rows = pl.ds(pl.multiple_of(y * 512, 512), 512)
        gds["far", d] = links.send(gd.at[j], far_gd.at[rows], device(x + 2, y + d, z, c))
        if d:
            gds["own", d] = links.send(gd.at[j], own_gd.at[rows], device(x, y + d, z, c))
        else:
            own_gd[rows, :] = gd[j]
    give(NCH - 1)
    so_id = links.send(so, so_far, far)
    so_own[...] = so[...]

    for (i, j), k in back.items():
        links.arrived(k, ret.at[lax.rem(x + 3 - i, 4) * 4 + lax.rem(inner + 4 - j, 4)])
    before = lax.broadcasted_iota(jnp.int32, (TOK, TOK), 0) < lax.broadcasted_iota(jnp.int32, (TOK, TOK), 1)
    places = jnp.dot((comb[...] > 0).astype(BF), before.astype(F32).astype(BF), preferred_element_type=F32)
    spots = lax.broadcasted_iota(jnp.int32, (CAP, TOK), 0).astype(F32)
    total = jnp.zeros((TOK, 256), F32)
    for e in range(BLK):
        weight = comb[e:e + 1, :]
        hit = (places[e:e + 1, :] == spots) & (weight > 0)
        spread = jnp.where(hit, 1.0, 0.0).astype(BF)
        total += lax.dot_general(spread, ret[e], TN, preferred_element_type=F32) * comb_t[:, e:e + 1]
    mixed[...] = total.astype(BF)
    links.arrived(gi_id, gi_far)
    links.arrived(sc_id, sc_far)
    links.arrived(so_id, so_far)
    for d in (1, 2, 3, 0):
        from_y = lax.rem(y - d + 4, 4)
        rows = pl.ds(pl.multiple_of(from_y * 512, 512), 512)
        links.arrived(gds["far", d], far_gd.at[rows])
        if d:
            links.arrived(gds["own", d], own_gd.at[rows])
    links.finish()


def down(hid, gi, sc, comb, comb_t, rg, di4, wd4, sd):
    n = 80
    vm = pl.BlockSpec(memory_space=pltpu.VMEM)
    return pl.pallas_call(
        down_kernel,
        out_shape=(
            jax.ShapeDtypeStruct((TOK, 256), BF),
            jax.ShapeDtypeStruct((2048, 256), BF),
            jax.ShapeDtypeStruct((2048, 256), BF),
            jax.ShapeDtypeStruct((ROWS, 256), BF),
            jax.ShapeDtypeStruct((8, 128), F32),
            jax.ShapeDtypeStruct((8, 256), F32),
            jax.ShapeDtypeStruct((8, 256), F32),
        ),
        in_specs=[vm] * 9,
        out_specs=[vm] * 7,
        scratch_shapes=[
            pltpu.VMEM((ROWS, 512), BF),
            pltpu.VMEM((4, ROWS, 256), BF),
            pltpu.VMEM((3, ROWS, 256), BF),
            pltpu.VMEM((ROWS, 256), BF),
            pltpu.VMEM((BLK, CAP, 256), BF),
            pltpu.VMEM((4, 512, 256), BF),
            pltpu.VMEM((8, 256), F32),
            pltpu.SemaphoreType.DMA((n,)),
            pltpu.SemaphoreType.DMA((n,)),
        ],
        name="down",
        compiler_params=pltpu.CompilerParams(collective_id=1, has_side_effects=True, vmem_limit_bytes=VMEM_LIMIT),
    )(hid, gi, sc, comb, comb_t, rg, di4, wd4, sd)


def picks(cw):
    mask = cw > 0
    place_of = jnp.cumsum(mask.astype(jnp.int32), axis=1) - 1
    spots = jnp.arange(CAP, dtype=jnp.int32)
    return ((place_of[:, None, :] == spots[None, :, None]) & mask[:, None, :]).astype(BF)


def per_device(
    tokens, cotangent, routes, router_weight, w_gate, w_up, w_down,
    scale_gate, scale_up, scale_down, swapped,
):
    me = lax.axis_index("expert")
    ids = jnp.arange(BLK, dtype=jnp.int32)
    flag = jnp.sum(jnp.where(ids == me, swapped, 0)) == 1
    comb_t = jnp.sum(jnp.where(routes[:, :, None] == ids, router_weight[:, :, None], 0.0), axis=1)
    comb = comb_t.T
    toks, rg, di4, wd4, hg, cw_own, cw_par = gather(comb, cotangent, tokens, w_down[0], scale_down)
    rows_x = jnp.einsum("rct,rtd->rcd", picks(cw_own), toks, preferred_element_type=F32).astype(BF).reshape(ROWS, D)
    gate_pre = jnp.dot(rows_x, w_gate[0], preferred_element_type=F32)
    up_pre = jnp.dot(rows_x, w_up[0], preferred_element_type=F32)
    gate_scale = scale_gate.astype(F32)
    up_scale = scale_up.astype(F32)
    gate_act = gate_pre * gate_scale
    up_act = up_pre * up_scale
    sig = jax.nn.sigmoid(gate_act)
    silu = gate_act * sig
    hidden = (silu * up_act).astype(BF)
    gate_grad = hg * up_act * sig * (1.0 + gate_act * (1.0 - sig))
    up_grad = hg * silu
    sc = jnp.concatenate(
        [
            jnp.sum(gate_grad * gate_pre, axis=0, keepdims=True),
            jnp.sum(up_grad * up_pre, axis=0, keepdims=True),
            jnp.zeros((6, 128), F32),
        ]
    )
    gi = jnp.concatenate([(gate_grad * gate_scale).astype(BF), (up_grad * up_scale).astype(BF)], axis=1)
    mixed, gd_own, gd_far, gi_far, sc_far, so_own, so_far = down(
        hidden, gi, sc, comb, comb_t, rg, di4, wd4, scale_down
    )
    chosen = jnp.where(flag, gi_far, gi).reshape(BLK, CAP, 256)
    spread = jnp.einsum(
        "rct,rcf->rtf", picks(jnp.where(flag, cw_par, cw_own)), chosen, preferred_element_type=F32
    ).astype(BF)
    wgrad = lax.dot_general(toks.reshape(BLK * TOK, D), spread.reshape(BLK * TOK, 256), TN, preferred_element_type=F32).astype(BF)
    grad_down = jnp.where(flag, gd_far, gd_own)
    scale_in = jnp.where(flag, sc_far, sc)[0:2].astype(BF)
    scale_out = jnp.where(flag, so_far, so_own)[0:1].astype(BF)
    return mixed, wgrad[None, :, :128], wgrad[None, :, 128:], grad_down[None], scale_in[None], scale_out


def solution(mesh):
    in_specs = (
        P("expert", None),
        P("expert", "dp"),
        P("expert", None),
        P("expert", None),
        P("expert", None, "dp"),
        P("expert", None, "dp"),
        P("expert", None, "dp"),
        P("expert", "dp"),
        P("expert", "dp"),
        P("expert", "dp"),
        P(),
    )
    out_specs = (
        P("expert", "dp"),
        P("expert", None, "dp"),
        P("expert", None, "dp"),
        P("expert", None, "dp"),
        P("expert", None, "dp"),
        P("expert", "dp"),
    )
    return jax.shard_map(
        per_device, mesh=mesh, in_specs=in_specs, out_specs=out_specs, check_vma=False
    )
```

time: 433 us -> 223 us (0.52)
  waiting for transfers between devices: 310 us -> 0 us
  Pallas kernels: 0 us -> 172 us
  starting transfers between devices: 25.8 us -> 0 us
  matrix products: 53.1 us -> 32.8 us
  local copies, waits for them, and re-layouts: 17.2 us -> 3.73 us
  between operations: 14.8 us -> 1.39 us
    all_to_all x3 -> x0, waiting for transfers between devices: 223 us -> none  [the longest x1 210 us: per_device(): lax.all_to_all(send_x, 'expert', split_axis=1, concat_axis=0, tiled=True)]
    pallas_call x0 -> x2, Pallas kernels: none -> 172 us  [the longest x1 96.3 us: gather(): pl.pallas_call(gather_kernel, out_shape=(jax.ShapeDtypeStruct((BLK, TOK,...]
    all_gather x1 -> x0, waiting for transfers between devices: 55.5 us -> none  [per_device(): piece = lax.all_gather(hidden, 'dp', axis=2, tiled=True)]
    ppermute x5 -> x0, waiting for transfers between devices: 31.6 us -> none  [swapped_2(): return lax.ppermute(block, axis, route)]
    dot_general x10 -> x4, matrix products: 53.1 us -> 32.8 us  [the longest x1 12.7 us: per_device(): jnp.einsum('rct,rtd->rcd', picks(cw_own), toks, preferred_element_type=F32)]
    all_to_all x3 -> x0, starting transfers between devices: 18.4 us -> none  [the longest x1 7.17 us: per_device(): lax.all_to_all(send_grad, 'expert', split_axis=1, concat_axis=0, tiled=True)]
    convert_element_type x4 -> x0, local copies, waits for them, and re-layouts: 15.2 us -> none  [the longest x1 13.7 us: per_device(): jnp.einsum('cet,td->ced', placed_b, tokens, preferred_element_type=jnp.fl...]
    ppermute x5 -> x0, starting transfers between devices: 7.16 us -> none  [swapped_2(): return lax.ppermute(block, axis, route)]
  transfers between devices with their start and end apart: 10 -> 0, of which waited for: 6 -> 0; matrix products, arithmetic and copies ran while one was open for 14% -> 0% of each run, Pallas kernels for 0% -> 0%
where the time goes in v1:
time: 223 us; the launch traced here: 222 us
  Pallas kernels  172 us (77%)
  matrix products  32.8 us (15%)
  other arithmetic  12.1 us (5%)
  local copies, waits for them, and re-layouts  3.73 us (2%)
    pallas_call x1, Pallas kernels, gather(): pl.pallas_call(gather_kernel, out_shape=(jax.ShapeDtypeStruct((BLK, TOK,...  96.3 us
    pallas_call x1, Pallas kernels, down(): pl.pallas_call(down_kernel, out_shape=(jax.ShapeDtypeStruct((TOK, 256), B...  75.8 us
    dot_general x1, matrix products, per_device(): jnp.einsum('rct,rtd->rcd', picks(cw_own), toks, preferred_element_type=F32)  12.7 us
    dot_general x1, matrix products, per_device(): lax.dot_general(toks.reshape(BLK * TOK, D), spread.reshape(BLK * TOK, 256...  9.41 us
    dot_general x1, matrix products, per_device(): up_pre = jnp.dot(rows_x, w_up[0], preferred_element_type=F32)  6.77 us

profile of v1, /device:TPU:1, one launch (start us, length us, event | category | flops | bytes accessed | tf_op | source)
XLA Modules:
  0.0 222.1 jit_solution(7709326781866243489)
XLA Ops:
  0.6 0.0 copy-start
  0.6 1.4 select_reduce_fusion
  2.0 96.3 %gather.1 = (bf16[16,128,4096]{2,1,0:T(8,128)(2,1)}, bf16[1280,256]{1,0:T(8,128)(2,1)}, bf16[4,1280,256]{2,1,0:T(8,128)(2,1)}, bf16[4,512,256]{2,1,0:T(8,128)(2,...) custom-call(f32[16,128]{1,0:T(8,128)} %bitcast.41, bf16[128,256]{1,0:T(8,128)(2,1)} %cot.1, ...), custom_call_target="tpu_custom_call" | custom-call | tf_op jit(solution)/shard_map/gather/pallas_call | solution.py:281
  98.4 1.3 fusion.18
  100.3 0.7 fusion.19
  101.1 0.3 reduce_window_sum.17
  101.3 0.0 copy-start.6
  101.4 12.7 %convolution_convert_fusion = bf16[16,80,4096]{2,1,0:T(8,128)(2,1)} fusion(bf16[16,128,4096]{2,1,0:T(8,128)(2,1)} %get-tuple-element.21, s32[16,128]{1,0:T(8,128)S(1)} %broadcast_add_fusion.1, pred[16,128]{1,0:T(8,128)(4,1)S(1)} %get-tuple-element.46), kind=kOutput, calls=%fused_computation | convolution fusion | flops 1347747840 | bytes 27273216 | tf_op jit(solution)/shard_map/rct,rtd->rcd/dot_general | solution.py:471
  114.1 0.0 copy-done.6
  114.1 6.8 %fusion.1 = f32[1280,128]{1,0:T(8,128)S(1)} fusion(bf16[1280,4096]{1,0:T(8,128)(2,1)} %bitcast.37, bf16[1,4096,128]{2,1,0:T(8,128)(2,1)S(1)} %copy-done.6), kind=kOutput, calls=%fused_computation.6 | convolution fusion | flops 1342177280 | bytes 12189696 | tf_op jit(solution)/shard_map/dot_general | solution.py:473
  120.9 0.0 copy-done.4
  120.9 0.0 copy-done.5
  120.9 0.0 copy-done
  120.9 0.2 copy-done.1
  121.1 0.1 copy-done.7
  121.2 3.9 %multiply_reduce_fusion.1 = (f32[128]{0:T(128)S(1)}, f32[128]{0:T(128)S(1)}, f32[1280,128]{1,0:T(8,128)S(1)}, bf16[1280,128]{1,0:T(8,128)(2,1)}, bf16[1280,128]{1,0:T(8,128)(2,1)S(1)}) fusion(f32[1280,128]{1,0:T(8,128)S(1)} %fusion.1, f32[1280,128]{1,0:T(8,128)S(1)} %copy-done.7, f32[128]{0:T(128)S(1)} %get-tuple-element.48, f32[128]{0:T(128)S(1)} %get-tuple-element.47, ...), kind=kOutput, calls=%fused_computation.14 | convolution fusion | flops 1345617664 | bytes 14157824 | tf_op jit(solution)/shard_map/dot_general | solution.py:472
  125.2 0.1 pad.2.clone
  125.2 0.7 maximum_maximum_fusion.sc
  125.9 0.9 pad_maximum_fusion.gi
  126.9 0.0 copy-done.2
  126.9 0.7 copy.22.comb_t
  127.6 75.8 %down.1 = (bf16[128,256]{1,0:T(8,128)(2,1)}, bf16[2048,256]{1,0:T(8,128)(2,1)}, bf16[2048,256]{1,0:T(8,128)(2,1)}, bf16[1280,256]{1,0:T(8,128)(2,1)}, f32[8,128]...) custom-call(bf16[1280,128]{1,0:T(8,128)(2,1)} %get-tuple-element.43.hid, bf16[1280,256]{1,0:T(8,128)(2,1)} %pad_maximum_fusion.gi, ...), custom_call_target="tpu_custom_call" | custom-call | tf_op jit(solution)/shard_map/down/pallas_call | solution.py:425
  203.4 1.3 fusion.17
  204.7 0.7 select_convert_fusion
  205.4 0.5 slice_bitcast_fusion.2
  205.9 2.3 %select_bitcast_fusion = bf16[1,2048,256]{2,1,0:T(8,128)(2,1)} fusion(bf16[2048,256]{1,0:T(8,128)(2,1)} %get-tuple-element.29, bf16[2048,256]{1,0:T(8,128)(2,1)} %get-tuple-element.30, pred[]{:T(512)S(6)} %eq.56), kind=kLoop, calls=%fused_computation.10 | loop fusion | flops 524288 | bytes 3145729 | tf_op jit(solution)/shard_map/broadcast_in_dim | solution.py:502
  208.2 2.1 broadcast_select_fusion
  210.3 0.3 reduce_window_sum.18
  210.6 9.4 %fusion = bf16[4096,256]{1,0:T(8,128)(2,1)S(1)} fusion(bf16[16,128,4096]{2,1,0:T(8,128)(2,1)} %get-tuple-element.21, bf16[16,80,256]{2,1,0:T(8,128)(2,1)} %bitcast.40, s32[16,128]{1,0:T(8,128)S(1)} %broadcast_add_fusion, pred[16,128]{1,0:T(8,128)(4,1)S(1)} %get-tuple-element.37), kind=kOutput, calls=%fused_computation.2 | convolution fusion | flops 4380753920 | bytes 19539968 | tf_op jit(solution)/shard_map/dot_general | solution.py:498
  220.0 1.5 slice_bitcast_fusion
  221.5 0.0 copy-done.3
  221.5 0.6 copy.26
  (11 shorter events, 0.1 us)
Async XLA Ops:
  0.6 120.3 %copy-start = (bf16[1,4096,128]{2,1,0:T(8,128)(2,1)S(1)}, bf16[1,4096,128]{2,1,0:T(8,128)(2,1)}, u32[]{:S(2)}) copy-start(bf16[1,4096,128]{2,1,0:T(8,128)(2,1)} %param.15) | copy-start | bytes 3145732
  101.3 12.7 %copy-start.6 = (bf16[1,4096,128]{2,1,0:T(8,128)(2,1)S(1)}, bf16[1,4096,128]{2,1,0:T(8,128)(2,1)}, u32[]{:S(2)}) copy-start(bf16[1,4096,128]{2,1,0:T(8,128)(2,1)} %param.16) | copy-start | bytes 3145732
  114.1 6.8 %copy-start.4 = (bf16[1,128]{1,0:T(2,128)(2,1)S(1)}, bf16[1,128]{1,0:T(2,128)(2,1)}, u32[]{:S(2)}) copy-start(bf16[1,128]{1,0:T(2,128)(2,1)} %param.19) | copy-start | bytes 772
  114.1 6.8 %copy-start.5 = (bf16[1,128]{1,0:T(2,128)(2,1)S(1)}, bf16[1,128]{1,0:T(2,128)(2,1)}, u32[]{:S(2)}) copy-start(bf16[1,128]{1,0:T(2,128)(2,1)} %param.18) | copy-start | bytes 772
  114.1 7.1 %copy-start.1 = (bf16[16,80,4096]{2,1,0:T(8,128)(2,1)S(1)}, bf16[16,80,4096]{2,1,0:T(8,128)(2,1)}, u32[]{:S(2)}) copy-start(bf16[16,80,4096]{2,1,0:T(8,128)(2,1)} %convolution_convert_fusion) | copy-start | bytes 31457284
  114.1 7.1 %copy-start.7 = (f32[1280,128]{1,0:T(8,128)S(1)}, f32[1280,128]{1,0:T(8,128)}, u32[]{:S(2)}) copy-start(f32[1280,128]{1,0:T(8,128)} %get-tuple-element.22) | copy-start | bytes 1966084
  121.2 5.6 %copy-start.2 = (f32[128,16]{0,1:T(8,128)S(1)}, f32[128,16]{0,1:T(8,128)}, u32[]{:S(2)}) copy-start(f32[128,16]{0,1:T(8,128)} %select_reduce_fusion) | copy-start | bytes 24580
  210.6 10.9 %copy-start.3 = (bf16[128,256]{1,0:T(8,128)(2,1)S(1)}, bf16[128,256]{1,0:T(8,128)(2,1)}, u32[]{:S(2)}) copy-start(bf16[128,256]{1,0:T(8,128)(2,1)} %get-tuple-element.55) | copy-start | bytes 196612

commit v2 on v0

v2 whole, which is shorter than its diff:
```python
import jax
import jax.numpy as jnp
from jax import lax
from jax.experimental import pallas as pl
from jax.experimental.pallas import tpu as pltpu
from jax.sharding import PartitionSpec as P

MESH = pl.DeviceIdType.MESH
BF = jnp.bfloat16
F32 = jnp.float32
CAP = 80
BLK = 16
TOK = 128
D = 4096
ROWS = BLK * CAP
CROWS = ROWS // 4
VMEM_LIMIT = 60 * 2**20
NT = (((1,), (1,)), ((), ()))
TN = (((0,), (0,)), ((), ()))


def place():
    dp = lax.axis_index("dp")
    ex = lax.axis_index("expert")
    y, zh = lax.div(dp, 4), lax.rem(dp, 4)
    x, zl, c = lax.div(ex, 4), lax.rem(lax.div(ex, 2), 2), lax.rem(ex, 2)
    return x, y, zh * 2 + zl, c


def device(x, y, z, c):
    x, y, z, c = lax.rem(x + 4, 4), lax.rem(y + 4, 4), lax.rem(z + 8, 8), lax.rem(c + 2, 2)
    return (y * 4 + lax.div(z, 2), slot(x, z, c))


def slot(x, z, c):
    return lax.rem(x + 4, 4) * 4 + lax.rem(z + 8, 2) * 2 + c


class Links:
    def __init__(self, send_sems, recv_sems, other):
        self.ss, self.rs, self.other = send_sems, recv_sems, other
        self.copies = []

    def send(self, src, dst, to):
        i = len(self.copies)
        copy = pltpu.make_async_remote_copy(
            src_ref=src,
            dst_ref=dst,
            send_sem=self.ss.at[i],
            recv_sem=self.rs.at[i],
            device_id=to,
            device_id_type=MESH,
        )
        copy.start()
        self.copies.append(copy)
        return i

    def arrived(self, i, dst):
        pltpu.make_async_remote_copy(
            src_ref=dst,
            dst_ref=dst,
            send_sem=self.ss.at[i],
            recv_sem=self.rs.at[i],
            device_id=self.other,
            device_id_type=MESH,
        ).wait_recv()

    def finish(self):
        for copy in self.copies:
            copy.wait_send()


def greet(devices):
    barrier = pltpu.get_barrier_semaphore()
    for to in devices:
        pl.semaphore_signal(barrier, inc=1, device_id=to, device_id_type=MESH)
    pl.semaphore_wait(barrier, len(devices))


def layer_kernel(
    comb, comb_t, cot, tok, wg, wu, wd, sg, su, sd, flag,
    mixed, grad_t, own_gd, far_gd, sc, sc_far, so, so_far,
    toks, w_in, cots, combs, cw_own, cw_par, pos, rg, di4, wd4, part, rz,
    pre, hid, hz, hz_t, op, ro, eo, ret, gd, gi, gi_far, spread_t, ss, rs, local,
):
    x, y, z, c = place()
    zl = lax.rem(z, 2)
    zh = lax.div(z, 2)
    me = slot(x, z, c)
    inner = lax.rem(me, 4)
    dp = lax.axis_index("dp")
    sibling = device(x, y, z, 1 - c)
    far = device(x + 2, y, z, c)
    up, down = device(x, y, z + 1, c), device(x, y, z - 1, c)
    chip = x * 2 + zl
    links = Links(ss, rs, sibling)

    def chip_at(k):
        q = lax.rem(chip + k + 8, 8)
        return lax.div(q, 2), zh * 2 + lax.rem(q, 2)

    def columns(j):
        return pl.ds(pl.multiple_of(j * 128, 128), 128)

    def quarter(j):
        return pl.ds(pl.multiple_of(j * 512, 512), 512)

    def chunk(j):
        return pl.ds(pl.multiple_of(j * CROWS, CROWS), CROWS)

    def block(r):
        return pl.ds(pl.multiple_of(r * CAP, CAP), CAP)

    loads = [
        pltpu.make_async_copy(tok, toks.at[me], local.at[0]),
        pltpu.make_async_copy(wg, w_in.at[:, pl.ds(0, 128)], local.at[1]),
        pltpu.make_async_copy(wu, w_in.at[:, pl.ds(128, 128)], local.at[2]),
    ]
    for load in loads:
        load.start()

    peers = [(dp, lax.rem(me + k, 16)) for k in range(1, 16)]
    peers.append(device(x, y, z - 1 + 2 * zl, c))
    for d in range(1, 4):
        peers.append(device(x, y + d, z, c))
        peers.append(device(x, y, z + 2 * d, c))
        peers.append(device(x + 2, y + d, z, c))
    greet(peers)

    first = []
    for k in range(1, 8):
        qx, qz = chip_at(k)
        to = device(qx, y, qz, c)
        first.append((k, links.send(comb, combs.at[me], to), links.send(cot, cots.at[me], to)))
    over = [(0, links.send(comb, combs.at[me], sibling), links.send(cot, cots.at[me], sibling))]
    wd_ids = []
    for d in (1, 3, 2):
        wd_ids.append((d, links.send(wd.at[quarter(lax.rem(y + d, 4))], wd4.at[y], device(x, y + d, z, c))))

    lower, upper = pl.ds(0, 64), pl.ds(64, 64)
    third, fourth = pl.ds(64, 32), pl.ds(96, 32)
    pair = {}

    def to_sibling(d, dz, rows):
        s = slot(x - d, z + dz, c)
        pair.setdefault((d, dz), []).append((links.send(toks.at[s, rows], toks.at[s, rows], sibling), rows))

    pair[0, 0] = [(links.send(tok, toks.at[me], sibling), pl.ds(0, TOK))]
    z_ids, x_ids = {}, {}
    z_ids[0] = (
        links.send(tok.at[lower], toks.at[me, lower], up),
        links.send(tok.at[upper], toks.at[me, upper], down),
    )
    for rows, name in ((upper, "u"), (lower, "l")):
        for d in (1, 3):
            x_ids[d, name] = links.send(tok.at[rows], toks.at[me, rows], device(x + d, y, z, c))

    combs[me] = comb[...]
    cots[me] = cot[...]
    wd4[y] = wd[quarter(y), :]
    for k, ia, ib in first:
        qx, qz = chip_at(-k)
        s = slot(qx, qz, c)
        links.arrived(ia, combs.at[s])
        links.arrived(ib, cots.at[s])
        over.append((k, links.send(combs.at[s], combs.at[s], sibling), links.send(cots.at[s], cots.at[s], sibling)))
    for k, ia, ib in over:
        qx, qz = chip_at(-k)
        s = slot(qx, qz, 1 - c)
        links.arrived(ia, combs.at[s])
        links.arrived(ib, cots.at[s])

    experts = lax.broadcasted_iota(jnp.int32, (BLK, BLK, TOK), 1)
    table = combs[...]
    cw = jnp.sum(jnp.where(experts == me, table, 0.0), axis=1)
    cw_own[...] = cw
    cw_par[...] = jnp.sum(jnp.where(experts == lax.rem(me + 8, 16), table, 0.0), axis=1)
    before = (
        lax.broadcasted_iota(jnp.int32, (TOK, TOK), 0) < lax.broadcasted_iota(jnp.int32, (TOK, TOK), 1)
    ).astype(F32).astype(BF)
    pos[...] = jnp.dot((cw > 0).astype(BF), before, preferred_element_type=F32)
    spots = lax.broadcasted_iota(jnp.int32, (CAP, TOK), 0).astype(F32)
    down_scale = sd[...].astype(F32)

    def compact(r, _):
        weight = cw_own[pl.ds(r, 1), :]
        hit = (pos[pl.ds(r, 1), :] == spots) & (weight > 0)
        picked = jnp.dot(jnp.where(hit, 1.0, 0.0).astype(BF), cots[r], preferred_element_type=F32)
        w = jnp.sum(jnp.where(hit, weight, 0.0), axis=1, keepdims=True)
        routed = (picked * w).astype(BF)
        rg[block(r), :] = routed
        di4[y, block(r), :] = (routed.astype(F32) * down_scale).astype(BF)
        return 0

    y_ids = {}
    for i in range(4):
        lax.fori_loop(i * 4, i * 4 + 4, compact, 0)
        rows = pl.ds(i * CROWS, CROWS)
        for d in (1, 3, 2):
            y_ids[i, d] = links.send(di4.at[y, rows], di4.at[y, rows], device(x, y + d, z, c))
    for d, i in wd_ids:
        links.arrived(i, wd4.at[lax.rem(y - d + 4, 4)])

    zr = {}

    def terms(i):
        rows = pl.ds(i * CROWS, CROWS)
        for d in (1, 3, 2):
            links.arrived(y_ids[i, d], di4.at[lax.rem(y - d + 4, 4), rows])
        acc = lax.dot_general(di4[0, rows, :], wd4[0], NT, preferred_element_type=F32)
        for j in range(1, 4):
            acc += lax.dot_general(di4[j, rows, :], wd4[j], NT, preferred_element_type=F32)
        acc = acc.astype(BF)
        for j in range(4):
            part[j, rows, :] = acc[:, j * 128:(j + 1) * 128]
        for d in (2, 1, 3):
            zr[i, d] = links.send(part.at[lax.rem(zh + d, 4), rows], rz.at[d - 1, rows], device(x, y, z + 2 * d, c))

    def z_own():
        s = slot(x, z + 1, c)
        links.arrived(z_ids[0][0], toks.at[s, lower])
        for d in (1, 3):
            x_ids[d, "z"] = links.send(toks.at[s, lower], toks.at[s, lower], device(x + d, y, z, c))
        to_sibling(0, 1, lower)
        links.arrived(z_ids[0][1], toks.at[s, upper])
        to_sibling(0, 1, upper)

    def x_near():
        for d in (1, 3):
            s = slot(x - d, z, c)
            links.arrived(x_ids[d, "u"], toks.at[s, upper])
            z_ids[d] = (
                links.send(toks.at[s, third], toks.at[s, third], up),
                links.send(toks.at[s, fourth], toks.at[s, fourth], down),
            )
            to_sibling(d, 0, upper)
        for rows, name in ((lower, "l"), (upper, "u")):
            x_ids[2, name] = links.send(tok.at[rows], toks.at[me, rows], far)
        for d in (1, 3):
            s = slot(x - d, z, c)
            links.arrived(x_ids[d, "l"], toks.at[s, lower])
            to_sibling(d, 0, lower)

    def near_rest():
        for d in (1, 3):
            s = slot(x - d, z + 1, c)
            links.arrived(x_ids[d, "z"], toks.at[s, lower])
            to_sibling(d, 1, lower)
        for d in (1, 3):
            s = slot(x - d, z + 1, c)
            links.arrived(z_ids[d][0], toks.at[s, third])
            links.arrived(z_ids[d][1], toks.at[s, fourth])
            to_sibling(d, 1, upper)

    def x_far():
        s = slot(x + 2, z, c)
        links.arrived(x_ids[2, "l"], toks.at[s, lower])
        a = links.send(toks.at[s, lower], toks.at[s, lower], up)
        to_sibling(2, 0, lower)
        links.arrived(x_ids[2, "u"], toks.at[s, upper])
        b = links.send(toks.at[s, upper], toks.at[s, upper], down)
        to_sibling(2, 0, upper)
        z_ids[2] = (a, b)

    def z_far():
        s = slot(x + 2, z + 1, c)
        links.arrived(z_ids[2][0], toks.at[s, lower])
        to_sibling(2, 1, lower)
        links.arrived(z_ids[2][1], toks.at[s, upper])
        to_sibling(2, 1, upper)

    gate_scale = sg[...].astype(F32)
    up_scale = su[...].astype(F32)
    hid_ids = {}

    def group(d):
        gx = lax.rem(x - d + 4, 4)
        for dz in (0, 1):
            s = slot(x - d, z + dz, 1 - c)
            for i, rows in pair[d, dz]:
                links.arrived(i, toks.at[s, rows])

        def deepen(k, acc):
            at = pl.ds(pl.multiple_of(k * 1024, 1024), 1024)
            left = toks[pl.ds(gx * 4, 4), :, at].reshape(4 * TOK, 1024)
            return acc + jnp.dot(left, w_in[at, :], preferred_element_type=F32)

        acc = lax.fori_loop(0, 4, deepen, jnp.zeros((4 * TOK, 256), F32))
        for j in range(4):
            r = gx * 4 + j
            hit = (pos[pl.ds(r, 1), :] == spots) & (cw_own[pl.ds(r, 1), :] > 0)
            pre[block(r), :] = jnp.dot(
                jnp.where(hit, 1.0, 0.0), acc[j * TOK:(j + 1) * TOK], precision=lax.Precision.HIGHEST,
                preferred_element_type=F32,
            )
        rows = chunk(gx)
        gate_act = pre[rows, 0:128] * gate_scale
        up_act = pre[rows, 128:256] * up_scale
        hid[rows, :] = (gate_act * jax.nn.sigmoid(gate_act) * up_act).astype(BF)
        hz[rows, columns(zh)] = hid[rows, :]
        for dz in (2, 1, 3):
            hid_ids[d, dz] = links.send(hid.at[rows], hz.at[rows, columns(zh)], device(x, y, z + 2 * dz, c))

    out_ids = {}

    def project(d):
        rows = chunk(lax.rem(x - d + 4, 4))
        for dz in (1, 3, 2):
            links.arrived(hid_ids[d, dz], hz.at[rows, columns(lax.rem(zh - dz + 4, 4))])
        left = hz[rows, :]
        for dy in (2, 1, 3, 0):
            j = lax.rem(y + dy, 4)
            op[j, rows, :] = jnp.dot(left, wd4[j], preferred_element_type=F32).astype(BF)
            if dy:
                out_ids[d, dy] = links.send(op.at[j, rows], ro.at[dy - 1, rows], device(x, y + dy, z, c))

    so[...] = jnp.zeros_like(so)
    back = {}

    def give(d):
        gx = lax.rem(x - d + 4, 4)
        rows = chunk(gx)
        for dy in (1, 3, 2):
            links.arrived(out_ids[d, dy], ro.at[dy - 1, rows])
        total = op[y, rows, :].astype(F32)
        for dy in (1, 2, 3):
            total += ro[dy - 1, rows, :].astype(F32)
        so[0:1, :] += jnp.sum(total * rg[rows, :].astype(F32), axis=0, keepdims=True)
        eo[rows, :] = (total * down_scale).astype(BF)
        for j in range(4):
            r = gx * 4 + lax.rem(inner + j, 4)
            if d == 0 and j == 0:
                ret[me] = eo[block(r), :]
            else:
                back[d, j] = links.send(eo.at[block(r)], ret.at[me], (dp, r))

    sc[...] = jnp.zeros_like(sc)
    gi_ids = {}

    def gradient(i):
        rows = pl.ds(i * CROWS, CROWS)
        for d in (1, 2, 3):
            links.arrived(zr[i, d], rz.at[d - 1, rows])
        total = part[zh, rows, :].astype(F32)
        for d in (1, 2, 3):
            total += rz[d - 1, rows, :].astype(F32)
        gate_pre, up_pre = pre[rows, 0:128], pre[rows, 128:256]
        gate_act, up_act = gate_pre * gate_scale, up_pre * up_scale
        sig = jax.nn.sigmoid(gate_act)
        gate_grad = total * up_act * sig * (1.0 + gate_act * (1.0 - sig))
        up_grad = total * (gate_act * sig)
        sc[0:1, :] += jnp.sum(gate_grad * gate_pre, axis=0, keepdims=True)
        sc[1:2, :] += jnp.sum(up_grad * up_pre, axis=0, keepdims=True)
        gi[rows, 0:128] = (gate_grad * gate_scale).astype(BF)
        gi[rows, 128:256] = (up_grad * up_scale).astype(BF)
        gi_ids[i] = links.send(gi.at[rows], gi_far.at[rows], far)

    for load in loads:
        load.wait()
    z_own()
    group(0)
    terms(0)
    x_near()
    terms(1)
    near_rest()
    terms(2)
    group(1)
    group(3)
    terms(3)
    x_far()
    project(0)
    z_far()
    group(2)
    project(1)
    give(0)
    for i in range(4):
        gradient(i)
    sc_id = links.send(sc, sc_far, far)
    project(3)
    give(1)
    project(2)

    hz_t[...] = hz[...].T
    gd_ids = {}
    for d in (2, 1, 3, 0):
        j = lax.rem(y + d, 4)
        gd[j] = jnp.dot(hz_t[...], di4[j], preferred_element_type=F32).astype(BF)
        gd_ids["far", d] = links.send(gd.at[j], far_gd.at[quarter(y)], device(x + 2, y + d, z, c))
        if d:
            gd_ids["own", d] = links.send(gd.at[j], own_gd.at[quarter(y)], device(x, y + d, z, c))
        else:
            own_gd[quarter(y), :] = gd[j]
    give(3)
    give(2)
    so_id = links.send(so, so_far, far)

    for i in range(4):
        links.arrived(gi_ids[i], gi_far.at[pl.ds(i * CROWS, CROWS)])
    trade = flag[...] > 0
    cw_sel = jnp.where(trade[:, 0:128], cw_par[...], cw_own[...])
    cw_par[...] = cw_sel
    pos[...] = jnp.dot((cw_sel > 0).astype(BF), before, preferred_element_type=F32)

    def expand(r, _):
        hit = (pos[pl.ds(r, 1), :] == spots) & (cw_par[pl.ds(r, 1), :] > 0)
        chosen = jnp.where(trade, gi_far[block(r), :].astype(F32), gi[block(r), :].astype(F32)).astype(BF)
        spread_t[:, columns(r)] = lax.dot_general(
            chosen, jnp.where(hit, 1.0, 0.0).astype(BF), TN, preferred_element_type=F32
        ).astype(BF)
        return 0

    lax.fori_loop(0, BLK, expand, 0)

    def weight_grad(k, _):
        at = pl.ds(pl.multiple_of(k * 512, 512), 512)
        right = toks[:, :, at].reshape(BLK * TOK, 512)
        grad_t[:, at] = jnp.dot(spread_t[...], right, preferred_element_type=F32).astype(BF)
        return 0

    lax.fori_loop(0, D // 512, weight_grad, 0)

    for (d, j), k in back.items():
        links.arrived(k, ret.at[lax.rem(x + d, 4) * 4 + lax.rem(inner + 4 - j, 4)])
    places = jnp.dot((comb[...] > 0).astype(BF), before, preferred_element_type=F32)
    total = jnp.zeros((TOK, 256), F32)
    for e in range(BLK):
        hit = (places[e:e + 1, :] == spots) & (comb[e:e + 1, :] > 0)
        total += (
            lax.dot_general(jnp.where(hit, 1.0, 0.0).astype(BF), ret[e], TN, preferred_element_type=F32)
            * comb_t[:, e:e + 1]
        )
    mixed[...] = total.astype(BF)
    links.arrived(sc_id, sc_far)
    links.arrived(so_id, so_far)
    for d in (1, 2, 3, 0):
        rows = quarter(lax.rem(y - d + 4, 4))
        links.arrived(gd_ids["far", d], far_gd.at[rows])
        if d:
            links.arrived(gd_ids["own", d], own_gd.at[rows])
    links.finish()


def layer(*args):
    n = 160
    vm = pl.BlockSpec(memory_space=pltpu.VMEM)
    hbm = pl.BlockSpec(memory_space=pl.ANY)
    return pl.pallas_call(
        layer_kernel,
        out_shape=(
            jax.ShapeDtypeStruct((TOK, 256), BF),
            jax.ShapeDtypeStruct((256, D), BF),
            jax.ShapeDtypeStruct((2048, 256), BF),
            jax.ShapeDtypeStruct((2048, 256), BF),
            jax.ShapeDtypeStruct((8, 128), F32),
            jax.ShapeDtypeStruct((8, 128), F32),
            jax.ShapeDtypeStruct((8, 256), F32),
            jax.ShapeDtypeStruct((8, 256), F32),
        ),
        in_specs=[vm, vm, vm, hbm, hbm, hbm, vm, vm, vm, vm, vm],
        out_specs=[vm] * 8,
        scratch_shapes=[
            pltpu.VMEM((BLK, TOK, D), BF),
            pltpu.VMEM((D, 256), BF),
            pltpu.VMEM((BLK, TOK, 256), BF),
            pltpu.VMEM((BLK, BLK, TOK), F32),
            pltpu.VMEM((BLK, TOK), F32),
            pltpu.VMEM((BLK, TOK), F32),
            pltpu.VMEM((BLK, TOK), F32),
            pltpu.VMEM((ROWS, 256), BF),
            pltpu.VMEM((4, ROWS, 256), BF),
            pltpu.VMEM((4, 512, 256), BF),
            pltpu.VMEM((4, ROWS, 128), BF),
            pltpu.VMEM((3, ROWS, 128), BF),
            pltpu.VMEM((ROWS, 256), F32),
            pltpu.VMEM((ROWS, 128), BF),
            pltpu.VMEM((ROWS, 512), BF),
            pltpu.VMEM((512, ROWS), BF),
            pltpu.VMEM((4, ROWS, 256), BF),
            pltpu.VMEM((3, ROWS, 256), BF),
            pltpu.VMEM((ROWS, 256), BF),
            pltpu.VMEM((BLK, CAP, 256), BF),
            pltpu.VMEM((4, 512, 256), BF),
            pltpu.VMEM((ROWS, 256), BF),
            pltpu.VMEM((ROWS, 256), BF),
            pltpu.VMEM((256, BLK * TOK), BF),
            pltpu.SemaphoreType.DMA((n,)),
            pltpu.SemaphoreType.DMA((n,)),
            pltpu.SemaphoreType.DMA((3,)),
        ],
        name="layer",
        compiler_params=pltpu.CompilerParams(collective_id=0, has_side_effects=True, vmem_limit_bytes=VMEM_LIMIT),
    )(*args)


def per_device(
    tokens, cotangent, routes, router_weight, w_gate, w_up, w_down,
    scale_gate, scale_up, scale_down, swapped,
):
    me = lax.axis_index("expert")
    ids = jnp.arange(BLK, dtype=jnp.int32)
    flag = jnp.sum(jnp.where(ids == me, swapped, 0)) == 1
    comb_t = jnp.sum(jnp.where(routes[:, :, None] == ids, router_weight[:, :, None], 0.0), axis=1)
    mixed, grad_t, gd_own, gd_far, sc, sc_far, so_own, so_far = layer(
        comb_t.T, comb_t, cotangent, tokens, w_gate[0], w_up[0], w_down[0],
        scale_gate, scale_up, scale_down, jnp.where(flag, jnp.ones((1, 256), F32), 0.0),
    )
    wgrad = grad_t.T
    grad_down = jnp.where(flag, gd_far, gd_own)
    scale_in = jnp.where(flag, sc_far, sc)[0:2].astype(BF)
    scale_out = jnp.where(flag, so_far, so_own)[0:1].astype(BF)
    return mixed, wgrad[None, :, :128], wgrad[None, :, 128:], grad_down[None], scale_in[None], scale_out


def solution(mesh):
    in_specs = (
        P("expert", None),
        P("expert", "dp"),
        P("expert", None),
        P("expert", None),
        P("expert", None, "dp"),
        P("expert", None, "dp"),
        P("expert", None, "dp"),
        P("expert", "dp"),
        P("expert", "dp"),
        P("expert", "dp"),
        P(),
    )
    out_specs = (
        P("expert", "dp"),
        P("expert", None, "dp"),
        P("expert", None, "dp"),
        P("expert", None, "dp"),
        P("expert", None, "dp"),
        P("expert", "dp"),
    )
    return jax.shard_map(
        per_device, mesh=mesh, in_specs=in_specs, out_specs=out_specs, check_vma=False
    )
```

time: 433 us -> 186 us (0.43)
  waiting for transfers between devices: 310 us -> 0 us
  Pallas kernels: 0 us -> 173 us
  matrix products: 53.1 us -> 0 us
  starting transfers between devices: 25.8 us -> 0 us
  between operations: 14.8 us -> 1.35 us
  local copies, waits for them, and re-layouts: 17.2 us -> 5.2 us
  other arithmetic: 11.2 us -> 5.76 us
    all_to_all x3 -> x0, waiting for transfers between devices: 223 us -> none  [the longest x1 210 us: per_device(): lax.all_to_all(send_x, 'expert', split_axis=1, concat_axis=0, tiled=True)]
    pallas_call x0 -> x1, Pallas kernels: none -> 173 us  [layer(): pl.pallas_call(layer_kernel, out_shape=(jax.ShapeDtypeStruct((TOK, 256),...]
    all_gather x1 -> x0, waiting for transfers between devices: 55.5 us -> none  [per_device(): piece = lax.all_gather(hidden, 'dp', axis=2, tiled=True)]
    dot_general x10 -> x0, matrix products: 53.1 us -> none  [the longest x1 8.58 us: per_device(): jnp.einsum('rjd,jdf->rjf', recv_x, w_gate, preferred_element_type=jnp.flo...]
    ppermute x5 -> x0, waiting for transfers between devices: 31.6 us -> none  [swapped_2(): return lax.ppermute(block, axis, route)]
    all_to_all x3 -> x0, starting transfers between devices: 18.4 us -> none  [the longest x1 7.17 us: per_device(): lax.all_to_all(send_grad, 'expert', split_axis=1, concat_axis=0, tiled=True)]
    convert_element_type x4 -> x0, local copies, waits for them, and re-layouts: 15.2 us -> none  [the longest x1 13.7 us: per_device(): jnp.einsum('cet,td->ced', placed_b, tokens, preferred_element_type=jnp.fl...]
    ppermute x5 -> x0, starting transfers between devices: 7.16 us -> none  [swapped_2(): return lax.ppermute(block, axis, route)]
  transfers between devices with their start and end apart: 10 -> 0, of which waited for: 6 -> 0; matrix products, arithmetic and copies ran while one was open for 14% -> 0% of each run, Pallas kernels for 0% -> 0%
where the time goes in v2:
time: 186 us; the launch traced here: 185 us
  Pallas kernels  173 us (93%)
  other arithmetic  5.76 us (3%)
  local copies, waits for them, and re-layouts  5.2 us (3%)
    pallas_call x1, Pallas kernels, layer(): pl.pallas_call(layer_kernel, out_shape=(jax.ShapeDtypeStruct((TOK, 256),...  173 us

profile of v2, /device:TPU:1, one launch (start us, length us, event | category | flops | bytes accessed | tf_op | source)
XLA Modules:
  0.0 185.1 jit_solution(9140682909280534419)
XLA Ops:
  0.6 1.3 fusion.1
  2.6 0.6 select_n.43.flag
  3.1 0.7 select_reduce_fusion
  3.9 0.0 copy-start.1
  3.9 0.7 copy.22.comb_t
  4.6 0.0 copy-done.1
  4.6 172.8 %layer.1 = (bf16[128,256]{1,0:T(8,128)(2,1)}, bf16[256,4096]{1,0:T(8,128)(2,1)}, bf16[2048,256]{1,0:T(8,128)(2,1)}, bf16[2048,256]{1,0:T(8,128)(2,1)}, f32[8,128...) custom-call(f32[16,128]{1,0:T(8,128)} %bitcast.17, f32[128,16]{1,0:T(8,128)} %copy.22.comb_t, ...), custom_call_target="tpu_custom_call" | custom-call | tf_op jit(solution)/shard_map/layer/pallas_call | solution.py:447
  177.4 0.0 copy-start.3
  177.4 0.0 copy-start.4
  177.4 0.0 copy-start
  177.5 2.5 %select_bitcast_fusion = bf16[1,2048,256]{2,1,0:T(8,128)(2,1)} fusion(bf16[2048,256]{1,0:T(8,128)(2,1)} %get-tuple-element.16, bf16[2048,256]{1,0:T(8,128)(2,1)} %get-tuple-element.17, pred[]{:T(512)S(6)} %eq.27), kind=kLoop, calls=%fused_computation.2 | loop fusion | flops 524288 | bytes 3145729 | tf_op jit(solution)/shard_map/broadcast_in_dim | solution.py:511
  179.9 0.0 copy-done.3
  179.9 0.0 copy-done.4
  179.9 0.5 slice_bitcast_fusion.2
  180.4 1.3 fusion
  181.7 0.0 copy-done
  181.7 0.1 slice_bitcast_fusion
  181.9 0.0 copy-start.2
  181.9 1.3 copy.23
  183.2 1.3 copy.24
  184.5 0.0 copy-done.2
  184.5 0.6 copy.26
  (1 shorter events, 0.0 us)
Async XLA Ops:
  3.9 0.7 copy-start.1
  177.4 2.5 %copy-start.3 = (f32[8,128]{1,0:T(8,128)S(1)}, f32[8,128]{1,0:T(8,128)}, u32[]{:S(2)}) copy-start(f32[8,128]{1,0:T(8,128)} %get-tuple-element.19) | copy-start | bytes 12292
  177.4 2.5 %copy-start.4 = (f32[8,128]{1,0:T(8,128)S(1)}, f32[8,128]{1,0:T(8,128)}, u32[]{:S(2)}) copy-start(f32[8,128]{1,0:T(8,128)} %get-tuple-element.18) | copy-start | bytes 12292
  177.4 4.3 %copy-start = (bf16[256,4096]{1,0:T(8,128)(2,1)S(1)}, bf16[256,4096]{1,0:T(8,128)(2,1)}, u32[]{:S(2)}) copy-start(bf16[256,4096]{1,0:T(8,128)(2,1)} %get-tuple-element.15) | copy-start | bytes 6291460
  181.9 2.6 %copy-start.2 = (bf16[128,256]{1,0:T(8,128)(2,1)S(1)}, bf16[128,256]{1,0:T(8,128)(2,1)}, u32[]{:S(2)}) copy-start(bf16[128,256]{1,0:T(8,128)(2,1)} %get-tuple-element.42) | copy-start | bytes 196612

commit v3 on v2

--- a/solution.py
+++ b/solution.py
@@ -14,6 +14,7 @@
 D = 4096
 ROWS = BLK * CAP
 CROWS = ROWS // 4
+ORDER = (0, 1, 3, 2)
 VMEM_LIMIT = 60 * 2**20
 NT = (((1,), (1,)), ((), ()))
 TN = (((0,), (0,)), ((), ()))
@@ -78,8 +79,9 @@
 
 
 def layer_kernel(
-    comb, comb_t, cot, tok, wg, wu, wd, sg, su, sd, flag,
-    mixed, grad_t, own_gd, far_gd, sc, sc_far, so, so_far,
+    routes, weights, cot, tok, wg, wu, wd, sg, su, sd, swapped,
+    mixed, grad_gate, grad_up, grad_down, grad_in, grad_out,
+    comb, comb_t, own_gd, far_gd, sc, sc_far, so, so_far,
     toks, w_in, cots, combs, cw_own, cw_par, pos, rg, di4, wd4, part, rz,
     pre, hid, hz, hz_t, op, ro, eo, ret, gd, gi, gi_far, spread_t, ss, rs, local,
 ):
@@ -119,6 +121,13 @@
     for load in loads:
         load.start()
 
+    names = lax.broadcasted_iota(jnp.int32, (TOK, TOK), 0)
+    dense = jnp.zeros((TOK, TOK), F32)
+    for k in range(routes.shape[0]):
+        dense += jnp.where(routes[k:k + 1, :] == names, weights[k:k + 1, :], 0.0)
+    comb[...] = dense[0:BLK]
+    comb_t[...] = dense.T
+
     peers = [(dp, lax.rem(me + k, 16)) for k in range(1, 16)]
     peers.append(device(x, y, z - 1 + 2 * zl, c))
     for d in range(1, 4):
@@ -138,22 +147,19 @@
         wd_ids.append((d, links.send(wd.at[quarter(lax.rem(y + d, 4))], wd4.at[y], device(x, y + d, z, c))))
 
     lower, upper = pl.ds(0, 64), pl.ds(64, 64)
-    third, fourth = pl.ds(64, 32), pl.ds(96, 32)
+    halves = {"l": lower, "u": upper}
     pair = {}
 
     def to_sibling(d, dz, rows):
         s = slot(x - d, z + dz, c)
         pair.setdefault((d, dz), []).append((links.send(toks.at[s, rows], toks.at[s, rows], sibling), rows))
 
+    z_ids, x_ids, f_ids = {}, {}, {}
+    z_ids["l"] = links.send(tok.at[lower], toks.at[me, lower], up)
+    z_ids["u"] = links.send(tok.at[upper], toks.at[me, upper], down)
+    for d, h in ((1, "l"), (3, "u"), (1, "u"), (3, "l")):
+        x_ids[d, 0, h] = links.send(tok.at[halves[h]], toks.at[me, halves[h]], device(x + d, y, z, c))
     pair[0, 0] = [(links.send(tok, toks.at[me], sibling), pl.ds(0, TOK))]
-    z_ids, x_ids = {}, {}
-    z_ids[0] = (
-        links.send(tok.at[lower], toks.at[me, lower], up),
-        links.send(tok.at[upper], toks.at[me, upper], down),
-    )
-    for rows, name in ((upper, "u"), (lower, "l")):
-        for d in (1, 3):
-            x_ids[d, name] = links.send(tok.at[rows], toks.at[me, rows], device(x + d, y, z, c))
 
     combs[me] = comb[...]
     cots[me] = cot[...]
@@ -192,21 +198,35 @@
         di4[y, block(r), :] = (routed.astype(F32) * down_scale).astype(BF)
         return 0
 
+    def rows_of(d, part=None):
+        start = lax.rem(x - d + 4, 4) * CROWS
+        if part is None:
+            return pl.ds(pl.multiple_of(start, CROWS), CROWS)
+        return pl.ds(pl.multiple_of(start + part * (CROWS // 2), CROWS // 2), CROWS // 2)
+
     y_ids = {}
-    for i in range(4):
-        lax.fori_loop(i * 4, i * 4 + 4, compact, 0)
-        rows = pl.ds(i * CROWS, CROWS)
-        for d in (1, 3, 2):
-            y_ids[i, d] = links.send(di4.at[y, rows], di4.at[y, rows], device(x, y + d, z, c))
+    for g in ORDER:
+        at = lax.rem(x - g + 4, 4) * 4
+        lax.fori_loop(at, at + 4, compact, 0)
+        rows = rows_of(g)
+        for d in (1, 3):
+            y_ids[g, d] = links.send(di4.at[y, rows], di4.at[y, rows], device(x, y + d, z, c))
     for d, i in wd_ids:
         links.arrived(i, wd4.at[lax.rem(y - d + 4, 4)])
 
+    def y_fwd(g):
+        for d, h in ((1, 0), (3, 1)):
+            j = lax.rem(y - d + 4, 4)
+            links.arrived(y_ids[g, d], di4.at[j, rows_of(g)])
+            rows = rows_of(g, h)
+            y_ids[g, d, "f"] = links.send(di4.at[j, rows], di4.at[j, rows], device(x, y + d, z, c))
+
     zr = {}
 
-    def terms(i):
-        rows = pl.ds(i * CROWS, CROWS)
-        for d in (1, 3, 2):
-            links.arrived(y_ids[i, d], di4.at[lax.rem(y - d + 4, 4), rows])
+    def terms(g):
+        rows = rows_of(g)
+        for d, h in ((1, 0), (3, 1)):
+            links.arrived(y_ids[g, d, "f"], di4.at[lax.rem(y + 2, 4), rows_of(g, h)])
         acc = lax.dot_general(di4[0, rows, :], wd4[0], NT, preferred_element_type=F32)
         for j in range(1, 4):
             acc += lax.dot_general(di4[j, rows, :], wd4[j], NT, preferred_element_type=F32)
@@ -214,60 +234,36 @@
         for j in range(4):
             part[j, rows, :] = acc[:, j * 128:(j + 1) * 128]
         for d in (2, 1, 3):
-            zr[i, d] = links.send(part.at[lax.rem(zh + d, 4), rows], rz.at[d - 1, rows], device(x, y, z + 2 * d, c))
+            zr[g, d] = links.send(part.at[lax.rem(zh + d, 4), rows], rz.at[d - 1, rows], device(x, y, z + 2 * d, c))
 
     def z_own():
         s = slot(x, z + 1, c)
-        links.arrived(z_ids[0][0], toks.at[s, lower])
-        for d in (1, 3):
-            x_ids[d, "z"] = links.send(toks.at[s, lower], toks.at[s, lower], device(x + d, y, z, c))
-        to_sibling(0, 1, lower)
-        links.arrived(z_ids[0][1], toks.at[s, upper])
-        to_sibling(0, 1, upper)
-
-    def x_near():
-        for d in (1, 3):
-            s = slot(x - d, z, c)
-            links.arrived(x_ids[d, "u"], toks.at[s, upper])
-            z_ids[d] = (
-                links.send(toks.at[s, third], toks.at[s, third], up),
-                links.send(toks.at[s, fourth], toks.at[s, fourth], down),
-            )
-            to_sibling(d, 0, upper)
-        for rows, name in ((lower, "l"), (upper, "u")):
-            x_ids[2, name] = links.send(tok.at[rows], toks.at[me, rows], far)
-        for d in (1, 3):
-            s = slot(x - d, z, c)
-            links.arrived(x_ids[d, "l"], toks.at[s, lower])
-            to_sibling(d, 0, lower)
-
-    def near_rest():
-        for d in (1, 3):
-            s = slot(x - d, z + 1, c)
-            links.arrived(x_ids[d, "z"], toks.at[s, lower])
-            to_sibling(d, 1, lower)
-        for d in (1, 3):
-            s = slot(x - d, z + 1, c)
-            links.arrived(z_ids[d][0], toks.at[s, third])
-            links.arrived(z_ids[d][1], toks.at[s, fourth])
-            to_sibling(d, 1, upper)
-
-    def x_far():
-        s = slot(x + 2, z, c)
-        links.arrived(x_ids[2, "l"], toks.at[s, lower])
-        a = links.send(toks.at[s, lower], toks.at[s, lower], up)
-        to_sibling(2, 0, lower)
-        links.arrived(x_ids[2, "u"], toks.at[s, upper])
-        b = links.send(toks.at[s, upper], toks.at[s, upper], down)
-        to_sibling(2, 0, upper)
-        z_ids[2] = (a, b)
-
-    def z_far():
-        s = slot(x + 2, z + 1, c)
-        links.arrived(z_ids[2][0], toks.at[s, lower])
-        to_sibling(2, 1, lower)
-        links.arrived(z_ids[2][1], toks.at[s, upper])
-        to_sibling(2, 1, upper)
+        for h, order in (("l", (1, 3)), ("u", (3, 1))):
+            rows = halves[h]
+            links.arrived(z_ids[h], toks.at[s, rows])
+            for d in order:
+                x_ids[d, 1, h] = links.send(toks.at[s, rows], toks.at[s, rows], device(x + d, y, z, c))
+            to_sibling(0, 1, rows)
+
+    def x_first(dz):
+        for d, h in ((1, "l"), (3, "u")):
+            s = slot(x - d, z + dz, c)
+            rows = halves[h]
+            links.arrived(x_ids[d, dz, h], toks.at[s, rows])
+            f_ids[d, dz] = links.send(toks.at[s, rows], toks.at[s, rows], device(x + d, y, z, c))
+            to_sibling(d, dz, rows)
+
+    def x_second(dz):
+        for d, h in ((1, "u"), (3, "l")):
+            s = slot(x - d, z + dz, c)
+            links.arrived(x_ids[d, dz, h], toks.at[s, halves[h]])
+            to_sibling(d, dz, halves[h])
+
+    def x_far(dz):
+        for d, h in ((1, "l"), (3, "u")):
+            s = slot(x + 2, z + dz, c)
+            links.arrived(f_ids[d, dz], toks.at[s, halves[h]])
+            to_sibling(2, dz, halves[h])
 
     gate_scale = sg[...].astype(F32)
     up_scale = su[...].astype(F32)
@@ -298,16 +294,24 @@
         up_act = pre[rows, 128:256] * up_scale
         hid[rows, :] = (gate_act * jax.nn.sigmoid(gate_act) * up_act).astype(BF)
         hz[rows, columns(zh)] = hid[rows, :]
-        for dz in (2, 1, 3):
+        for dz in (1, 3):
             hid_ids[d, dz] = links.send(hid.at[rows], hz.at[rows, columns(zh)], device(x, y, z + 2 * dz, c))
+
+    def hid_fwd(d):
+        for dz, h in ((1, 0), (3, 1)):
+            at = columns(lax.rem(zh - dz + 4, 4))
+            links.arrived(hid_ids[d, dz], hz.at[rows_of(d), at])
+            rows = rows_of(d, h)
+            hid_ids[d, dz, "f"] = links.send(hz.at[rows, at], hz.at[rows, at], device(x, y, z + 2 * dz, c))
 
     out_ids = {}
 
     def project(d):
         rows = chunk(lax.rem(x - d + 4, 4))
-        for dz in (1, 3, 2):
-            links.arrived(hid_ids[d, dz], hz.at[rows, columns(lax.rem(zh - dz + 4, 4))])
+        for dz, h in ((1, 0), (3, 1)):
+            links.arrived(hid_ids[d, dz, "f"], hz.at[rows_of(d, h), columns(lax.rem(zh + 2, 4))])
         left = hz[rows, :]
+        hz_t[lax.rem(x - d + 4, 4)] = left.T
         for dy in (2, 1, 3, 0):
             j = lax.rem(y + dy, 4)
             op[j, rows, :] = jnp.dot(left, wd4[j], preferred_element_type=F32).astype(BF)
@@ -337,10 +341,10 @@
     sc[...] = jnp.zeros_like(sc)
     gi_ids = {}
 
-    def gradient(i):
-        rows = pl.ds(i * CROWS, CROWS)
+    def gradient(g):
+        rows = rows_of(g)
         for d in (1, 2, 3):
-            links.arrived(zr[i, d], rz.at[d - 1, rows])
+            links.arrived(zr[g, d], rz.at[d - 1, rows])
         total = part[zh, rows, :].astype(F32)
         for d in (1, 2, 3):
             total += rz[d - 1, rows, :].astype(F32)
@@ -353,51 +357,70 @@
         sc[1:2, :] += jnp.sum(up_grad * up_pre, axis=0, keepdims=True)
         gi[rows, 0:128] = (gate_grad * gate_scale).astype(BF)
         gi[rows, 128:256] = (up_grad * up_scale).astype(BF)
-        gi_ids[i] = links.send(gi.at[rows], gi_far.at[rows], far)
+
+    def trade_gi(g):
+        gi_ids[g] = links.send(gi.at[rows_of(g)], gi_far.at[rows_of(g)], far)
 
     for load in loads:
         load.wait()
     z_own()
+    y_fwd(0)
     group(0)
+    x_first(0)
+    y_fwd(1)
     terms(0)
-    x_near()
+    y_fwd(3)
+    x_second(0)
     terms(1)
-    near_rest()
+    hid_fwd(0)
+    y_fwd(2)
+    x_first(1)
+    terms(3)
     terms(2)
+    project(0)
+    x_second(1)
+    x_far(0)
     group(1)
     group(3)
-    terms(3)
-    x_far()
-    project(0)
-    z_far()
+    hid_fwd(1)
+    hid_fwd(3)
+    gradient(0)
+    give(0)
+    gradient(1)
+    project(1)
+    gradient(3)
+    project(3)
+    x_far(1)
+    for g in (0, 1, 3):
+        trade_gi(g)
     group(2)
-    project(1)
-    give(0)
-    for i in range(4):
-        gradient(i)
-    sc_id = links.send(sc, sc_far, far)
-    project(3)
     give(1)
+    hid_fwd(2)
+    gradient(2)
     project(2)
 
-    hz_t[...] = hz[...].T
     gd_ids = {}
     for d in (2, 1, 3, 0):
         j = lax.rem(y + d, 4)
-        gd[j] = jnp.dot(hz_t[...], di4[j], preferred_element_type=F32).astype(BF)
+        acc = jnp.dot(hz_t[0], di4[j, 0:CROWS, :], preferred_element_type=F32)
+        for i in range(1, 4):
+            acc += jnp.dot(hz_t[i], di4[j, i * CROWS:(i + 1) * CROWS, :], preferred_element_type=F32)
+        gd[j] = acc.astype(BF)
         gd_ids["far", d] = links.send(gd.at[j], far_gd.at[quarter(y)], device(x + 2, y + d, z, c))
         if d:
             gd_ids["own", d] = links.send(gd.at[j], own_gd.at[quarter(y)], device(x, y + d, z, c))
         else:
             own_gd[quarter(y), :] = gd[j]
+    trade_gi(2)
+    sc_id = links.send(sc, sc_far, far)
     give(3)
     give(2)
     so_id = links.send(so, so_far, far)
 
-    for i in range(4):
-        links.arrived(gi_ids[i], gi_far.at[pl.ds(i * CROWS, CROWS)])
-    trade = flag[...] > 0
-    cw_sel = jnp.where(trade[:, 0:128], cw_par[...], cw_own[...])
+    for g in ORDER:
+        links.arrived(gi_ids[g], gi_far.at[rows_of((g + 2) % 4)])
+    trade = jnp.sum(jnp.where(lax.broadcasted_iota(jnp.int32, (1, BLK), 1) == me, swapped[...], 0), axis=1, keepdims=True) > 0
+    cw_sel = jnp.where(trade, cw_par[...], cw_own[...])
     cw_par[...] = cw_sel
     pos[...] = jnp.dot((cw_sel > 0).astype(BF), before, preferred_element_type=F32)
 
@@ -414,7 +437,9 @@
     def weight_grad(k, _):
         at = pl.ds(pl.multiple_of(k * 512, 512), 512)
         right = toks[:, :, at].reshape(BLK * TOK, 512)
-        grad_t[:, at] = jnp.dot(spread_t[...], right, preferred_element_type=F32).astype(BF)
+        grad = jnp.dot(spread_t[...], right, preferred_element_type=F32).astype(BF).T
+        grad_gate[at, :] = grad[:, 0:128]
+        grad_up[at, :] = grad[:, 128:256]
         return 0
 
     lax.fori_loop(0, D // 512, weight_grad, 0)
@@ -437,6 +462,9 @@
         links.arrived(gd_ids["far", d], far_gd.at[rows])
         if d:
             links.arrived(gd_ids["own", d], own_gd.at[rows])
+    grad_down[...] = jnp.where(trade, far_gd[...], own_gd[...])
+    grad_in[...] = jnp.where(trade, sc_far[0:2], sc[0:2]).astype(BF)
+    grad_out[...] = jnp.where(trade, so_far[0:1], so[0:1]).astype(BF)
     links.finish()
 
 
@@ -448,17 +476,23 @@
         layer_kernel,
         out_shape=(
             jax.ShapeDtypeStruct((TOK, 256), BF),
-            jax.ShapeDtypeStruct((256, D), BF),
+            jax.ShapeDtypeStruct((D, 128), BF),
+            jax.ShapeDtypeStruct((D, 128), BF),
             jax.ShapeDtypeStruct((2048, 256), BF),
-            jax.ShapeDtypeStruct((2048, 256), BF),
-            jax.ShapeDtypeStruct((8, 128), F32),
-            jax.ShapeDtypeStruct((8, 128), F32),
-            jax.ShapeDtypeStruct((8, 256), F32),
-            jax.ShapeDtypeStruct((8, 256), F32),
+            jax.ShapeDtypeStruct((2, 128), BF),
+            jax.ShapeDtypeStruct((1, 256), BF),
         ),
         in_specs=[vm, vm, vm, hbm, hbm, hbm, vm, vm, vm, vm, vm],
-        out_specs=[vm] * 8,
+        out_specs=[vm] * 6,
         scratch_shapes=[
+            pltpu.VMEM((BLK, TOK), F32),
+            pltpu.VMEM((TOK, TOK), F32),
+            pltpu.VMEM((2048, 256), BF),
+            pltpu.VMEM((2048, 256), BF),
+            pltpu.VMEM((8, 128), F32),
+            pltpu.VMEM((8, 128), F32),
+            pltpu.VMEM((8, 256), F32),
+            pltpu.VMEM((8, 256), F32),
             pltpu.VMEM((BLK, TOK, D), BF),
             pltpu.VMEM((D, 256), BF),
             pltpu.VMEM((BLK, TOK, 256), BF),
@@ -474,7 +508,7 @@
             pltpu.VMEM((ROWS, 256), F32),
             pltpu.VMEM((ROWS, 128), BF),
             pltpu.VMEM((ROWS, 512), BF),
-            pltpu.VMEM((512, ROWS), BF),
+            pltpu.VMEM((4, 512, CROWS), BF),
             pltpu.VMEM((4, ROWS, 256), BF),
             pltpu.VMEM((3, ROWS, 256), BF),
             pltpu.VMEM((ROWS, 256), BF),
@@ -496,19 +530,11 @@
     tokens, cotangent, routes, router_weight, w_gate, w_up, w_down,
     scale_gate, scale_up, scale_down, swapped,
 ):
-    me = lax.axis_index("expert")
-    ids = jnp.arange(BLK, dtype=jnp.int32)
-    flag = jnp.sum(jnp.where(ids == me, swapped, 0)) == 1
-    comb_t = jnp.sum(jnp.where(routes[:, :, None] == ids, router_weight[:, :, None], 0.0), axis=1)
-    mixed, grad_t, gd_own, gd_far, sc, sc_far, so_own, so_far = layer(
-        comb_t.T, comb_t, cotangent, tokens, w_gate[0], w_up[0], w_down[0],
-        scale_gate, scale_up, scale_down, jnp.where(flag, jnp.ones((1, 256), F32), 0.0),
+    mixed, grad_gate, grad_up, grad_down, grad_in, grad_out = layer(
+        routes.T, router_weight.T, cotangent, tokens, w_gate[0], w_up[0], w_down[0],
+        scale_gate, scale_up, scale_down, swapped[None],
     )
-    wgrad = grad_t.T
-    grad_down = jnp.where(flag, gd_far, gd_own)
-    scale_in = jnp.where(flag, sc_far, sc)[0:2].astype(BF)
-    scale_out = jnp.where(flag, so_far, so_own)[0:1].astype(BF)
-    return mixed, wgrad[None, :, :128], wgrad[None, :, 128:], grad_down[None], scale_in[None], scale_out
+    return mixed, grad_gate[None], grad_up[None], grad_down[None], grad_in[None], grad_out
 
 
 def solution(mesh):

time: 186 us -> 168 us (0.903)
  Pallas kernels: 173 us -> 159 us
  other arithmetic: 5.76 us -> 0 us
  local copies, waits for them, and re-layouts: 5.2 us -> 7.59 us
    pallas_call x1, Pallas kernels: 173 us -> 159 us  [layer(): pl.pallas_call(layer_kernel, out_shape=(jax.ShapeDtypeStruct((TOK, 256),...]
    unnamed x13 -> x14, local copies, waits for them, and re-layouts: 3.26 us -> 7.59 us
    broadcast_in_dim x1 -> x0, other arithmetic: 2.46 us -> none  [per_device(): grad_down[None]]
    reduce_sum x2 -> x0, other arithmetic: 2.01 us -> none  [the longest x1 1.29 us: per_device(): flag = jnp.sum(jnp.where(ids == me, swapped, 0)) == 1]
where the time goes in v3:
time: 168 us; the launch traced here: 167 us
  Pallas kernels  159 us (95%)
  local copies, waits for them, and re-layouts  7.59 us (5%)
    pallas_call x1, Pallas kernels, layer(): pl.pallas_call(layer_kernel, out_shape=(jax.ShapeDtypeStruct((TOK, 256),...  159 us
    unnamed x14, local copies, waits for them, and re-layouts  7.59 us

profile of v3, /device:TPU:1, one launch (start us, length us, event | category | flops | bytes accessed | tf_op | source)
XLA Modules:
  0.0 166.8 jit_solution(17194816458327414149)
XLA Ops:
  0.6 158.6 %layer.1 = (bf16[128,256]{1,0:T(8,128)(2,1)}, bf16[4096,128]{1,0:T(8,128)(2,1)}, bf16[4096,128]{1,0:T(8,128)(2,1)}, bf16[2048,256]{1,0:T(8,128)(2,1)}, bf16[2,128]{1,0:T(2,128)(2,1)}, /*index=5*/bf16[1,256]{1,0:T(2,128)(2,1)}) custom-call(s32[8,128]{1,0:T(8,128)} %bitcast.16, f32[8,128]{1,0:T(8,128)} %bitcast.17, bf16[128,256]{1,0:T(8,128)(2,1)} %cot.1, ...), custom_call_target="tpu_custom_call" | custom-call | tf_op jit(solution)/shard_map/layer/pallas_call | solution.py:475
  159.2 1.5 copy.23
  160.7 0.0 copy-start.1
  160.7 2.4 %copy.24 = bf16[1,4096,128]{2,1,0:T(8,128)(2,1)} copy(bf16[1,4096,128]{2,1,0:T(8,128)(2,1)} %bitcast.12) | data formatting | bytes 2097152
  163.0 0.0 copy-done.1
  163.0 0.0 copy-start
  163.0 1.0 copy.25
  164.0 0.6 copy-done
  164.6 0.0 copy-start.3
  164.6 1.0 copy.26
  165.6 0.0 copy-done.3
  165.6 0.0 copy-start.2
  165.6 0.5 copy.27
  166.1 0.1 copy-done.2
  166.2 0.6 copy.28
Async XLA Ops:
  160.7 2.4 %copy-start.1 = (bf16[4096,128]{1,0:T(8,128)(2,1)S(1)}, bf16[4096,128]{1,0:T(8,128)(2,1)}, u32[]{:S(2)}) copy-start(bf16[4096,128]{1,0:T(8,128)(2,1)} %get-tuple-element.14) | copy-start | bytes 3145732
  163.0 1.6 copy-start
  164.6 1.0 copy-start.3
  165.6 0.6 copy-start.2

commit v4 on v3

--- a/solution.py
+++ b/solution.py
@@ -15,6 +15,8 @@
 ROWS = BLK * CAP
 CROWS = ROWS // 4
 ORDER = (0, 1, 3, 2)
+XCOLS = 1280
+YCOLS = 384
 VMEM_LIMIT = 60 * 2**20
 NT = (((1,), (1,)), ((), ()))
 TN = (((0,), (0,)), ((), ()))
@@ -146,20 +148,26 @@
     for d in (1, 3, 2):
         wd_ids.append((d, links.send(wd.at[quarter(lax.rem(y + d, 4))], wd4.at[y], device(x, y + d, z, c))))
 
-    lower, upper = pl.ds(0, 64), pl.ds(64, 64)
-    halves = {"l": lower, "u": upper}
+    cols = {"l": pl.ds(0, XCOLS), "u": pl.ds(XCOLS, XCOLS)}
+    ylow, yhigh = pl.ds(2 * XCOLS, 2 * YCOLS), pl.ds(2 * XCOLS + 2 * YCOLS, 2 * YCOLS)
+    shared = pl.ds(2 * XCOLS, 4 * YCOLS)
+
+    def mine(d):
+        return pl.ds(pl.multiple_of(2 * XCOLS + lax.rem(y + d + 4, 4) * YCOLS, 128), YCOLS)
+
     pair = {}
 
-    def to_sibling(d, dz, rows):
+    def to_sibling(d, dz, at):
         s = slot(x - d, z + dz, c)
-        pair.setdefault((d, dz), []).append((links.send(toks.at[s, rows], toks.at[s, rows], sibling), rows))
-
-    z_ids, x_ids, f_ids = {}, {}, {}
-    z_ids["l"] = links.send(tok.at[lower], toks.at[me, lower], up)
-    z_ids["u"] = links.send(tok.at[upper], toks.at[me, upper], down)
-    for d, h in ((1, "l"), (3, "u"), (1, "u"), (3, "l")):
-        x_ids[d, 0, h] = links.send(tok.at[halves[h]], toks.at[me, halves[h]], device(x + d, y, z, c))
-    pair[0, 0] = [(links.send(tok, toks.at[me], sibling), pl.ds(0, TOK))]
+        pair.setdefault((d, dz), []).append((links.send(toks.at[s, :, at], toks.at[s, :, at], sibling), at))
+
+    z_ids, x_ids, f_ids, v_ids = {}, {}, {}, {}
+    for name, at, to in (("l", cols["l"], up), ("u", cols["u"], down), ("ylow", ylow, up), ("yhigh", yhigh, down)):
+        z_ids[name] = links.send(tok.at[:, at], toks.at[me, :, at], to)
+    for d, h in ((1, "l"), (3, "u"), (1, "q"), (3, "q"), (1, "u"), (3, "l")):
+        at = mine(0) if h == "q" else cols[h]
+        x_ids[d, 0, h] = links.send(tok.at[:, at], toks.at[me, :, at], device(x + d, y, z, c))
+    pair[0, 0] = [(links.send(tok, toks.at[me], sibling), pl.ds(0, D))]
 
     combs[me] = comb[...]
     cots[me] = cot[...]
@@ -238,32 +246,61 @@
 
     def z_own():
         s = slot(x, z + 1, c)
-        for h, order in (("l", (1, 3)), ("u", (3, 1))):
-            rows = halves[h]
-            links.arrived(z_ids[h], toks.at[s, rows])
-            for d in order:
-                x_ids[d, 1, h] = links.send(toks.at[s, rows], toks.at[s, rows], device(x + d, y, z, c))
-            to_sibling(0, 1, rows)
+        for name, at in (("l", cols["l"]), ("u", cols["u"]), ("ylow", ylow), ("yhigh", yhigh)):
+            links.arrived(z_ids[name], toks.at[s, :, at])
+        for d, h in ((1, "l"), (3, "u"), (1, "q"), (3, "q"), (1, "u"), (3, "l")):
+            at = mine(0) if h == "q" else cols[h]
+            x_ids[d, 1, h] = links.send(toks.at[s, :, at], toks.at[s, :, at], device(x + d, y, z, c))
+        to_sibling(0, 1, pl.ds(0, D))
 
     def x_first(dz):
         for d, h in ((1, "l"), (3, "u")):
             s = slot(x - d, z + dz, c)
-            rows = halves[h]
-            links.arrived(x_ids[d, dz, h], toks.at[s, rows])
-            f_ids[d, dz] = links.send(toks.at[s, rows], toks.at[s, rows], device(x + d, y, z, c))
-            to_sibling(d, dz, rows)
+            at = cols[h]
+            links.arrived(x_ids[d, dz, h], toks.at[s, :, at])
+            f_ids[d, dz] = links.send(toks.at[s, :, at], toks.at[s, :, at], device(x + d, y, z, c))
+            to_sibling(d, dz, at)
 
     def x_second(dz):
         for d, h in ((1, "u"), (3, "l")):
             s = slot(x - d, z + dz, c)
-            links.arrived(x_ids[d, dz, h], toks.at[s, halves[h]])
-            to_sibling(d, dz, halves[h])
+            links.arrived(x_ids[d, dz, h], toks.at[s, :, cols[h]])
+            to_sibling(d, dz, cols[h])
 
     def x_far(dz):
         for d, h in ((1, "l"), (3, "u")):
             s = slot(x + 2, z + dz, c)
-            links.arrived(f_ids[d, dz], toks.at[s, halves[h]])
-            to_sibling(2, dz, halves[h])
+            links.arrived(f_ids[d, dz], toks.at[s, :, cols[h]])
+            to_sibling(2, dz, cols[h])
+
+    def share(d, dz):
+        view = toks.at[slot(x - d, z + dz, c), :, mine(0)]
+        for dy in (1, 3):
+            v_ids[d, dz, dy] = links.send(view, view, device(x, y + dy, z, c))
+
+    def q_near(dz):
+        for d in (1, 3):
+            view = toks.at[slot(x - d, z + dz, c), :, mine(0)]
+            links.arrived(x_ids[d, dz, "q"], view)
+            if d == 1 + 2 * dz:
+                f_ids["q", dz] = links.send(view, view, device(x + d, y, z, c))
+            share(d, dz)
+
+    def q_far(dz):
+        links.arrived(f_ids["q", dz], toks.at[slot(x + 2, z + dz, c), :, mine(0)])
+        share(2, dz)
+
+    def v_pass(d, dz):
+        s = slot(x - d, z + dz, c)
+        for dy in (1, 3):
+            view = toks.at[s, :, mine(-dy)]
+            links.arrived(v_ids[d, dz, dy], view)
+            if dy == 1 + 2 * dz:
+                v_ids[d, dz, "f"] = links.send(view, view, device(x, y + dy, z, c))
+
+    def v_last(d, dz):
+        links.arrived(v_ids[d, dz, "f"], toks.at[slot(x - d, z + dz, c), :, mine(2)])
+        to_sibling(d, dz, shared)
 
     gate_scale = sg[...].astype(F32)
     up_scale = su[...].astype(F32)
@@ -273,8 +310,8 @@
         gx = lax.rem(x - d + 4, 4)
         for dz in (0, 1):
             s = slot(x - d, z + dz, 1 - c)
-            for i, rows in pair[d, dz]:
-                links.arrived(i, toks.at[s, rows])
+            for i, at in pair[d, dz]:
+                links.arrived(i, toks.at[s, :, at])
 
         def deepen(k, acc):
             at = pl.ds(pl.multiple_of(k * 1024, 1024), 1024)
@@ -367,23 +404,39 @@
     y_fwd(0)
     group(0)
     x_first(0)
+    q_near(0)
     y_fwd(1)
     terms(0)
+    q_far(0)
+    v_pass(1, 0)
+    v_pass(3, 0)
     y_fwd(3)
     x_second(0)
     terms(1)
     hid_fwd(0)
     y_fwd(2)
     x_first(1)
+    q_near(1)
+    v_pass(2, 0)
     terms(3)
+    q_far(1)
+    v_last(1, 0)
+    v_last(3, 0)
+    v_last(2, 0)
+    v_pass(1, 1)
+    v_pass(3, 1)
     terms(2)
     project(0)
     x_second(1)
+    v_pass(2, 1)
+    v_last(1, 1)
+    v_last(3, 1)
     x_far(0)
     group(1)
     group(3)
     hid_fwd(1)
     hid_fwd(3)
+    v_last(2, 1)
     gradient(0)
     give(0)
     gradient(1)
@@ -469,7 +522,7 @@
 
 
 def layer(*args):
-    n = 160
+    n = 220
     vm = pl.BlockSpec(memory_space=pltpu.VMEM)
     hbm = pl.BlockSpec(memory_space=pl.ANY)
     return pl.pallas_call(
@@ -526,14 +579,37 @@
     )(*args)
 
 
+def hand_over_kernel(*refs):
+    count = len(refs) // 2
+    sems = refs[-1]
+    copies = [pltpu.make_async_copy(refs[i], refs[count + i], sems.at[i]) for i in range(count)]
+    for copy in copies:
+        copy.start()
+    for copy in copies:
+        copy.wait()
+
+
+def hand_over(arrays):
+    hbm = pl.BlockSpec(memory_space=pl.ANY)
+    return pl.pallas_call(
+        hand_over_kernel,
+        out_shape=[jax.ShapeDtypeStruct(a.shape, a.dtype) for a in arrays],
+        in_specs=[hbm] * len(arrays),
+        out_specs=[hbm] * len(arrays),
+        scratch_shapes=[pltpu.SemaphoreType.DMA((len(arrays),))],
+        name="hand_over",
+        compiler_params=pltpu.CompilerParams(vmem_limit_bytes=VMEM_LIMIT),
+    )(*arrays)
+
+
 def per_device(
     tokens, cotangent, routes, router_weight, w_gate, w_up, w_down,
     scale_gate, scale_up, scale_down, swapped,
 ):
-    mixed, grad_gate, grad_up, grad_down, grad_in, grad_out = layer(
+    mixed, grad_gate, grad_up, grad_down, grad_in, grad_out = hand_over(layer(
         routes.T, router_weight.T, cotangent, tokens, w_gate[0], w_up[0], w_down[0],
         scale_gate, scale_up, scale_down, swapped[None],
-    )
+    ))
     return mixed, grad_gate[None], grad_up[None], grad_down[None], grad_in[None], grad_out
 
 

time: 168 us -> 270 us (1.61)
  the two profiles are of different devices: /device:TPU:1 before, /device:TPU:24 now
where the time goes in v4:
time: 270 us
  Pallas kernels  269 us (100%)
    pallas_call x1, Pallas kernels, layer(): pl.pallas_call(layer_kernel, out_shape=(jax.ShapeDtypeStruct((TOK, 256),...  171 us
    pallas_call x1, Pallas kernels, hand_over(): pl.pallas_call(hand_over_kernel, out_shape=[jax.ShapeDtypeStruct(a.shape,...  98.5 us

profile of v4, /device:TPU:24, one launch (start us, length us, event | category | flops | bytes accessed | tf_op | source)
XLA Modules:
  0.0 270.2 jit_solution(4809007100452153394)
XLA Ops:
  0.6 170.9 %layer.1 = (bf16[128,256]{1,0:T(8,128)(2,1)}, bf16[4096,128]{1,0:T(8,128)(2,1)}, bf16[4096,128]{1,0:T(8,128)(2,1)}, bf16[2048,256]{1,0:T(8,128)(2,1)}, bf16[2,128]{1,0:T(2,128)(2,1)}, /*index=5*/bf16[1,256]{1,0:T(2,128)(2,1)}) custom-call(s32[8,128]{1,0:T(8,128)} %bitcast.13, f32[8,128]{1,0:T(8,128)} %bitcast.14, bf16[128,256]{1,0:T(8,128)(2,1)} %cot.1, ...), custom_call_target="tpu_custom_call" | custom-call | tf_op jit(solution)/shard_map/layer/pallas_call | solution.py:528
  171.5 98.5 %hand_over.1 = (bf16[128,256]{1,0:T(8,128)(2,1)}, bf16[4096,128]{1,0:T(8,128)(2,1)}, bf16[4096,128]{1,0:T(8,128)(2,1)}, bf16[2048,256]{1,0:T(8,128)(2,1)}, bf16[...) custom-call(bf16[128,256]{1,0:T(8,128)(2,1)} %get-tuple-element.18.refs_0_, bf16[4096,128]{1,0:T(8,128)(2,1)} %get-tuple-element.19.refs_1_, ...), custom_call_target="tpu_custom_call" | custom-call | tf_op jit(solution)/shard_map/hand_over/pallas_call | solution.py:594

commit v5 on v3

--- a/solution.py
+++ b/solution.py
@@ -382,21 +382,20 @@
     x_far(0)
     group(1)
     group(3)
+    x_far(1)
     hid_fwd(1)
     hid_fwd(3)
+    group(2)
     gradient(0)
-    give(0)
     gradient(1)
-    project(1)
     gradient(3)
-    project(3)
-    x_far(1)
     for g in (0, 1, 3):
         trade_gi(g)
-    group(2)
-    give(1)
+    project(1)
+    project(3)
     hid_fwd(2)
     gradient(2)
+    trade_gi(2)
     project(2)
 
     gd_ids = {}
@@ -411,7 +410,8 @@
             gd_ids["own", d] = links.send(gd.at[j], own_gd.at[quarter(y)], device(x, y + d, z, c))
         else:
             own_gd[quarter(y), :] = gd[j]
-    trade_gi(2)
+    give(0)
+    give(1)
     sc_id = links.send(sc, sc_far, far)
     give(3)
     give(2)
@@ -526,14 +526,42 @@
     )(*args)
 
 
+def hand_over_kernel(*refs):
+    count = (len(refs) - 2) // 3
+    given, out, held = refs[:count], refs[count:2 * count], refs[2 * count:3 * count]
+    loads = [pltpu.make_async_copy(given[i], held[i], refs[-2].at[i]) for i in range(count)]
+    stores = [pltpu.make_async_copy(held[i], out[i], refs[-1].at[i]) for i in range(count)]
+    for load in loads:
+        load.start()
+    for load, store in zip(loads, stores):
+        load.wait()
+        store.start()
+    for store in stores:
+        store.wait()
+
+
+def hand_over(arrays):
+    hbm = pl.BlockSpec(memory_space=pl.ANY)
+    return pl.pallas_call(
+        hand_over_kernel,
+        out_shape=[jax.ShapeDtypeStruct(a.shape, a.dtype) for a in arrays],
+        in_specs=[hbm] * len(arrays),
+        out_specs=[hbm] * len(arrays),
+        scratch_shapes=[pltpu.VMEM(a.shape, a.dtype) for a in arrays]
+        + [pltpu.SemaphoreType.DMA((len(arrays),))] * 2,
+        name="hand_over",
+        compiler_params=pltpu.CompilerParams(vmem_limit_bytes=VMEM_LIMIT),
+    )(*arrays)
+
+
 def per_device(
     tokens, cotangent, routes, router_weight, w_gate, w_up, w_down,
     scale_gate, scale_up, scale_down, swapped,
 ):
-    mixed, grad_gate, grad_up, grad_down, grad_in, grad_out = layer(
+    mixed, grad_gate, grad_up, grad_down, grad_in, grad_out = hand_over(layer(
         routes.T, router_weight.T, cotangent, tokens, w_gate[0], w_up[0], w_down[0],
         scale_gate, scale_up, scale_down, swapped[None],
-    )
+    ))
     return mixed, grad_gate[None], grad_up[None], grad_down[None], grad_in[None], grad_out
 
 

time: 168 us -> 150 us (0.89)
  Pallas kernels: 159 us -> 149 us
  local copies, waits for them, and re-layouts: 7.59 us -> 0 us
    pallas_call x1, Pallas kernels: 159 us -> 146 us  [layer(): pl.pallas_call(layer_kernel, out_shape=(jax.ShapeDtypeStruct((TOK, 256),...]
    unnamed x14 -> x0, local copies, waits for them, and re-layouts: 7.59 us -> none
    pallas_call x0 -> x1, Pallas kernels: none -> 3.03 us  [hand_over(): pl.pallas_call(hand_over_kernel, out_shape=[jax.ShapeDtypeStruct(a.shape,...]
where the time goes in v5:
time: 150 us; the launch traced here: 149 us
  Pallas kernels  149 us (99%)
    pallas_call x1, Pallas kernels, layer(): pl.pallas_call(layer_kernel, out_shape=(jax.ShapeDtypeStruct((TOK, 256),...  146 us
    pallas_call x1, Pallas kernels, hand_over(): pl.pallas_call(hand_over_kernel, out_shape=[jax.ShapeDtypeStruct(a.shape,...  3.03 us

profile of v5, /device:TPU:1, one launch (start us, length us, event | category | flops | bytes accessed | tf_op | source)
XLA Modules:
  0.0 149.2 jit_solution(259320055232120537)
XLA Ops:
  0.6 145.5 %layer.1 = (bf16[128,256]{1,0:T(8,128)(2,1)}, bf16[4096,128]{1,0:T(8,128)(2,1)}, bf16[4096,128]{1,0:T(8,128)(2,1)}, bf16[2048,256]{1,0:T(8,128)(2,1)}, bf16[2,128]{1,0:T(2,128)(2,1)}, /*index=5*/bf16[1,256]{1,0:T(2,128)(2,1)}) custom-call(s32[8,128]{1,0:T(8,128)} %bitcast.13, f32[8,128]{1,0:T(8,128)} %bitcast.14, bf16[128,256]{1,0:T(8,128)(2,1)} %cot.1, ...), custom_call_target="tpu_custom_call" | custom-call | tf_op jit(solution)/shard_map/layer/pallas_call | solution.py:475
  146.2 3.0 %hand_over.1 = (bf16[128,256]{1,0:T(8,128)(2,1)}, bf16[4096,128]{1,0:T(8,128)(2,1)}, bf16[4096,128]{1,0:T(8,128)(2,1)}, bf16[2048,256]{1,0:T(8,128)(2,1)}, bf16[...) custom-call(bf16[128,256]{1,0:T(8,128)(2,1)} %get-tuple-element.18.refs_0_, bf16[4096,128]{1,0:T(8,128)(2,1)} %get-tuple-element.19.refs_1_, ...), custom_call_target="tpu_custom_call" | custom-call | tf_op jit(solution)/shard_map/hand_over/pallas_call | solution.py:545

commit v6 on v5

--- a/solution.py
+++ b/solution.py
@@ -157,9 +157,38 @@
     z_ids, x_ids, f_ids = {}, {}, {}
     z_ids["l"] = links.send(tok.at[lower], toks.at[me, lower], up)
     z_ids["u"] = links.send(tok.at[upper], toks.at[me, upper], down)
-    for d, h in ((1, "l"), (3, "u"), (1, "u"), (3, "l")):
+    for d, h in ((1, "l"), (3, "u")):
         x_ids[d, 0, h] = links.send(tok.at[halves[h]], toks.at[me, halves[h]], device(x + d, y, z, c))
     pair[0, 0] = [(links.send(tok, toks.at[me], sibling), pl.ds(0, TOK))]
+
+    def z_own():
+        s = slot(x, z + 1, c)
+        for h, order in (("l", (1, 3)), ("u", (3, 1))):
+            rows = halves[h]
+            links.arrived(z_ids[h], toks.at[s, rows])
+            for d in order:
+                x_ids[d, 1, h] = links.send(toks.at[s, rows], toks.at[s, rows], device(x + d, y, z, c))
+            to_sibling(0, 1, rows)
+
+    def x_first(dz):
+        for d, h in ((1, "l"), (3, "u")):
+            s = slot(x - d, z + dz, c)
+            rows = halves[h]
+            links.arrived(x_ids[d, dz, h], toks.at[s, rows])
+            f_ids[d, dz] = links.send(toks.at[s, rows], toks.at[s, rows], device(x + d, y, z, c))
+            to_sibling(d, dz, rows)
+
+    def x_second(dz):
+        for d, h in ((1, "u"), (3, "l")):
+            s = slot(x - d, z + dz, c)
+            links.arrived(x_ids[d, dz, h], toks.at[s, halves[h]])
+            to_sibling(d, dz, halves[h])
+
+    def x_far(dz):
+        for d, h in ((1, "l"), (3, "u")):
+            s = slot(x + 2, z + dz, c)
+            links.arrived(f_ids[d, dz], toks.at[s, halves[h]])
+            to_sibling(2, dz, halves[h])
 
     combs[me] = comb[...]
     cots[me] = cot[...]
@@ -170,6 +199,9 @@
         links.arrived(ia, combs.at[s])
         links.arrived(ib, cots.at[s])
         over.append((k, links.send(combs.at[s], combs.at[s], sibling), links.send(cots.at[s], cots.at[s], sibling)))
+    for d, h in ((1, "u"), (3, "l")):
+        x_ids[d, 0, h] = links.send(tok.at[halves[h]], toks.at[me, halves[h]], device(x + d, y, z, c))
+    z_own()
     for k, ia, ib in over:
         qx, qz = chip_at(-k)
         s = slot(qx, qz, 1 - c)
@@ -235,35 +267,6 @@
             part[j, rows, :] = acc[:, j * 128:(j + 1) * 128]
         for d in (2, 1, 3):
             zr[g, d] = links.send(part.at[lax.rem(zh + d, 4), rows], rz.at[d - 1, rows], device(x, y, z + 2 * d, c))
-
-    def z_own():
-        s = slot(x, z + 1, c)
-        for h, order in (("l", (1, 3)), ("u", (3, 1))):
-            rows = halves[h]
-            links.arrived(z_ids[h], toks.at[s, rows])
-            for d in order:
-                x_ids[d, 1, h] = links.send(toks.at[s, rows], toks.at[s, rows], device(x + d, y, z, c))
-            to_sibling(0, 1, rows)
-
-    def x_first(dz):
-        for d, h in ((1, "l"), (3, "u")):
-            s = slot(x - d, z + dz, c)
-            rows = halves[h]
-            links.arrived(x_ids[d, dz, h], toks.at[s, rows])
-            f_ids[d, dz] = links.send(toks.at[s, rows], toks.at[s, rows], device(x + d, y, z, c))
-            to_sibling(d, dz, rows)
-
-    def x_second(dz):
-        for d, h in ((1, "u"), (3, "l")):
-            s = slot(x - d, z + dz, c)
-            links.arrived(x_ids[d, dz, h], toks.at[s, halves[h]])
-            to_sibling(d, dz, halves[h])
-
-    def x_far(dz):
-        for d, h in ((1, "l"), (3, "u")):
-            s = slot(x + 2, z + dz, c)
-            links.arrived(f_ids[d, dz], toks.at[s, halves[h]])
-            to_sibling(2, dz, halves[h])
 
     gate_scale = sg[...].astype(F32)
     up_scale = su[...].astype(F32)
@@ -363,7 +366,6 @@
 
     for load in loads:
         load.wait()
-    z_own()
     y_fwd(0)
     group(0)
     x_first(0)
@@ -382,15 +384,15 @@
     x_far(0)
     group(1)
     group(3)
+    gradient(0)
+    gradient(1)
+    gradient(3)
     x_far(1)
+    for g in (0, 1, 3):
+        trade_gi(g)
     hid_fwd(1)
     hid_fwd(3)
     group(2)
-    gradient(0)
-    gradient(1)
-    gradient(3)
-    for g in (0, 1, 3):
-        trade_gi(g)
     project(1)
     project(3)
     hid_fwd(2)

time: 150 us -> 148 us (0.987)
  no operation moved by 1% of the time
where the time goes in v6:
time: 148 us
  Pallas kernels  148 us (100%)
    pallas_call x1, Pallas kernels, layer(): pl.pallas_call(layer_kernel, out_shape=(jax.ShapeDtypeStruct((TOK, 256),...  145 us
    pallas_call x1, Pallas kernels, hand_over(): pl.pallas_call(hand_over_kernel, out_shape=[jax.ShapeDtypeStruct(a.shape,...  3.03 us

profile of v6, /device:TPU:1, one launch (start us, length us, event | category | flops | bytes accessed | tf_op | source)
XLA Modules:
  0.0 148.3 jit_solution(7019751965865542519)
XLA Ops:
  0.6 144.6 %layer.1 = (bf16[128,256]{1,0:T(8,128)(2,1)}, bf16[4096,128]{1,0:T(8,128)(2,1)}, bf16[4096,128]{1,0:T(8,128)(2,1)}, bf16[2048,256]{1,0:T(8,128)(2,1)}, bf16[2,128]{1,0:T(2,128)(2,1)}, /*index=5*/bf16[1,256]{1,0:T(2,128)(2,1)}) custom-call(s32[8,128]{1,0:T(8,128)} %bitcast.13, f32[8,128]{1,0:T(8,128)} %bitcast.14, bf16[128,256]{1,0:T(8,128)(2,1)} %cot.1, ...), custom_call_target="tpu_custom_call" | custom-call | tf_op jit(solution)/shard_map/layer/pallas_call | solution.py:477
  145.2 3.0 %hand_over.1 = (bf16[128,256]{1,0:T(8,128)(2,1)}, bf16[4096,128]{1,0:T(8,128)(2,1)}, bf16[4096,128]{1,0:T(8,128)(2,1)}, bf16[2048,256]{1,0:T(8,128)(2,1)}, bf16[...) custom-call(bf16[128,256]{1,0:T(8,128)(2,1)} %get-tuple-element.18.refs_0_, bf16[4096,128]{1,0:T(8,128)(2,1)} %get-tuple-element.19.refs_1_, ...), custom_call_target="tpu_custom_call" | custom-call | tf_op jit(solution)/shard_map/hand_over/pallas_call | solution.py:547

commit v7 on v6

--- a/solution.py
+++ b/solution.py
@@ -531,8 +531,13 @@
 def hand_over_kernel(*refs):
     count = (len(refs) - 2) // 3
     given, out, held = refs[:count], refs[count:2 * count], refs[2 * count:3 * count]
-    loads = [pltpu.make_async_copy(given[i], held[i], refs[-2].at[i]) for i in range(count)]
-    stores = [pltpu.make_async_copy(held[i], out[i], refs[-1].at[i]) for i in range(count)]
+    parts = []
+    for i in range(count):
+        rows = given[i].shape[0]
+        cut = rows // 4 if rows >= 2048 else rows
+        parts += [(i, pl.ds(at, cut)) for at in range(0, rows, cut)]
+    loads = [pltpu.make_async_copy(given[i].at[r], held[i].at[r], refs[-2].at[n]) for n, (i, r) in enumerate(parts)]
+    stores = [pltpu.make_async_copy(held[i].at[r], out[i].at[r], refs[-1].at[n]) for n, (i, r) in enumerate(parts)]
     for load in loads:
         load.start()
     for load, store in zip(loads, stores):
@@ -550,7 +555,7 @@
         in_specs=[hbm] * len(arrays),
         out_specs=[hbm] * len(arrays),
         scratch_shapes=[pltpu.VMEM(a.shape, a.dtype) for a in arrays]
-        + [pltpu.SemaphoreType.DMA((len(arrays),))] * 2,
+        + [pltpu.SemaphoreType.DMA((4 * len(arrays),))] * 2,
         name="hand_over",
         compiler_params=pltpu.CompilerParams(vmem_limit_bytes=VMEM_LIMIT),
     )(*arrays)

time: 148 us -> 148 us (level)
  no operation moved by 1% of the time
where the time goes in v7:
time: 148 us
  Pallas kernels  148 us (100%)
    pallas_call x1, Pallas kernels, layer(): pl.pallas_call(layer_kernel, out_shape=(jax.ShapeDtypeStruct((TOK, 256),...  145 us
    pallas_call x1, Pallas kernels, hand_over(): pl.pallas_call(hand_over_kernel, out_shape=[jax.ShapeDtypeStruct(a.shape,...  3.07 us

profile of v7, /device:TPU:1, one launch (start us, length us, event | category | flops | bytes accessed | tf_op | source)
XLA Modules:
  0.0 148.3 jit_solution(15154651013263254391)
XLA Ops:
  0.6 144.6 %layer.1 = (bf16[128,256]{1,0:T(8,128)(2,1)}, bf16[4096,128]{1,0:T(8,128)(2,1)}, bf16[4096,128]{1,0:T(8,128)(2,1)}, bf16[2048,256]{1,0:T(8,128)(2,1)}, bf16[2,128]{1,0:T(2,128)(2,1)}, /*index=5*/bf16[1,256]{1,0:T(2,128)(2,1)}) custom-call(s32[8,128]{1,0:T(8,128)} %bitcast.13, f32[8,128]{1,0:T(8,128)} %bitcast.14, bf16[128,256]{1,0:T(8,128)(2,1)} %cot.1, ...), custom_call_target="tpu_custom_call" | custom-call | tf_op jit(solution)/shard_map/layer/pallas_call | solution.py:477
  145.2 3.1 %hand_over.1 = (bf16[128,256]{1,0:T(8,128)(2,1)}, bf16[4096,128]{1,0:T(8,128)(2,1)}, bf16[4096,128]{1,0:T(8,128)(2,1)}, bf16[2048,256]{1,0:T(8,128)(2,1)}, bf16[...) custom-call(bf16[128,256]{1,0:T(8,128)(2,1)} %get-tuple-element.18.refs_0_, bf16[4096,128]{1,0:T(8,128)(2,1)} %get-tuple-element.19.refs_1_, ...), custom_call_target="tpu_custom_call" | custom-call | tf_op jit(solution)/shard_map/hand_over/pallas_call | solution.py:552
